TPU v7x, 256 devices: a whole 4x4x8 slice. The times are simulated.
256 devices in a mesh: dp: 4 (over x), tm: 64 (over z, y, core).
Axes of the slice: x: 4, y: 4, z: 8, core: 2. Of those that a mesh axis runs over, the one named last changes fastest.
Arguments:
- queries: bfloat16 [512, 64, 1536], P(('dp', 'tm')), parts along dimension 0, may hold values from -6 to 6
- key_states: bfloat16 [512, 64, 1536], P(('dp', 'tm')), parts along dimension 0, may hold values from -6 to 6
- value_states: bfloat16 [512, 64, 1536], P(('dp', 'tm')), parts along dimension 0, may hold values from -6 to 6
- clip_ids: int32 [512], P(('dp', 'tm')), parts along dimension 0, may hold values from 0 to 7, never falling along the last dimension, each value on 1 to 80 neighbouring positions
Outputs:
- attended: bfloat16 [512, 64, 1536], P(('dp', 'tm')), parts along dimension 0
There are 4 independent parts, one for each index of `dp`. A program takes and returns all parts, laid end to end along the dimension named above; each array names one. Nothing has to cross between parts.
All inputs are finite; a program needn't handle non-finite values.
Results may differ from a plain program's by a relative error of at most 0.003.
Values may be sent and summed in bfloat16 or wider, within the bound.
A program may use at most 256 MiB of HBM per device.

v0:
```python
import jax
import jax.numpy as jnp
from jax import lax
from jax.sharding import PartitionSpec as P

HEAD_DIM = 64
SIDE = 8
NEAR = 2


def passed_along(value, axis, steps):
    count = lax.axis_size(axis)
    first, last = (max(0, -steps), min(count, count - steps))
    return lax.ppermute(value, axis, [(source, source + steps) for source in range(first, last)])


def pooled_grid(states, stride):
    frame_count = states.shape[0]
    cells = SIDE // stride
    grid = states.astype(jnp.float32).reshape(
        frame_count, cells, stride, cells, stride, states.shape[-1]
    )
    return (
        jnp.mean(grid, axis=(2, 4))
        .reshape(frame_count, cells * cells, states.shape[-1])
        .astype(jnp.bfloat16)
    )


def clip_lookup(frame_numbers, table):
    positions = jnp.arange(table.shape[0], dtype=jnp.int32)
    matches = frame_numbers[:, None] == positions[None, :]
    return jnp.sum(jnp.where(matches, table[None, :] + 1, 0), axis=1) - 1


def attend_block(
    carried,
    query_heads,
    query_frames,
    query_clips,
    block_keys,
    block_values,
    key_frames,
    key_clips,
    flavor,
):
    top_old, totals, summed = carried
    heads = query_heads.shape[1]
    key_heads = block_keys.reshape(block_keys.shape[0], heads, HEAD_DIM)
    value_heads = block_values.reshape(block_values.shape[0], heads, HEAD_DIM)
    scores = jnp.einsum(
        "qhe,khe->hqk", query_heads, key_heads, preferred_element_type=jnp.float32
    ) * HEAD_DIM ** (-0.5)
    distance = query_frames[:, None] - key_frames[None, :]
    same_clip = query_clips[:, None] == key_clips[None, :]
    if flavor == "own":
        allowed = distance == 0
    elif flavor == "near":
        allowed = same_clip & (distance >= 1) & (distance <= NEAR)
    else:
        allowed = same_clip & (distance > NEAR)
    scores = jnp.where(allowed[None], scores, -1e30)
    top_new = jnp.maximum(top_old, jnp.max(scores, axis=-1))
    weights = jnp.where(allowed[None], jnp.exp(scores - top_new[:, :, None]), 0.0)
    factor = jnp.exp(top_old - top_new)
    totals = totals * factor + jnp.sum(weights, axis=-1)
    update = jnp.einsum(
        "hqk,khe->qhe",
        weights.astype(jnp.bfloat16),
        value_heads,
        preferred_element_type=jnp.float32,
    )
    summed = summed * jnp.transpose(factor)[:, :, None] + update
    return (top_new, totals, summed)


def on_device(queries, key_states, value_states, clip_ids):
    fr_dev, tok, width = queries.shape
    heads = width // HEAD_DIM
    tm_size = lax.axis_size("tm")
    first_frame = lax.axis_index("tm") * fr_dev
    table = lax.all_gather(clip_ids, "tm", axis=0, tiled=True)
    local_frames = first_frame + jnp.arange(fr_dev, dtype=jnp.int32)
    rows_total = fr_dev * tok
    query_frames = jnp.repeat(local_frames, tok)
    query_clips = jnp.repeat(clip_ids, tok)
    query_heads = queries.reshape(rows_total, heads, HEAD_DIM)
    carried = (
        jnp.full((heads, rows_total), -1e30, jnp.float32),
        jnp.zeros((heads, rows_total), jnp.float32),
        jnp.zeros((rows_total, heads, HEAD_DIM), jnp.float32),
    )
    carried = attend_block(
        carried,
        query_heads,
        query_frames,
        query_clips,
        key_states.reshape(rows_total, width),
        value_states.reshape(rows_total, width),
        query_frames,
        query_clips,
        "own",
    )
    near_rows = (SIDE // 2) ** 2
    near_stack = jnp.stack(
        [
            pooled_grid(key_states, 2).reshape(fr_dev * near_rows, width),
            pooled_grid(value_states, 2).reshape(fr_dev * near_rows, width),
        ]
    )
    near_pieces = [near_stack]
    near_frames = [jnp.repeat(local_frames, near_rows)]
    near_pieces.append(passed_along(near_stack, "tm", 1))
    near_frames.append(jnp.repeat(local_frames - fr_dev, near_rows))
    near_all = jnp.concatenate(near_pieces, axis=1)
    near_numbers = jnp.concatenate(near_frames)
    carried = attend_block(
        carried,
        query_heads,
        query_frames,
        query_clips,
        near_all[0],
        near_all[1],
        near_numbers,
        clip_lookup(near_numbers, table),
        "near",
    )
    far_rows = (SIDE // 4) ** 2
    far_keys = pooled_grid(key_states, 4).reshape(fr_dev * far_rows, width)
    far_values = pooled_grid(value_states, 4).reshape(fr_dev * far_rows, width)
    span = fr_dev * tm_size * 5 // 8
    inner = carried
    piece_keys = lax.all_gather(far_keys, "tm", axis=0, tiled=True)
    piece_values = lax.all_gather(far_values, "tm", axis=0, tiled=True)
    rows_here = piece_keys.shape[0]
    block = rows_here
    while block > 512 and block % 2 == 0:
        block = block // 2

    def one_block(state, counter):
        start_row = counter * block
        lowest = start_row // far_rows
        highest = (start_row + block - 1) // far_rows
        useful = (highest >= first_frame - span) & (lowest <= first_frame + fr_dev - 2 - NEAR)

        def attend_here(current):
            numbers = (start_row + jnp.arange(block, dtype=jnp.int32)) // far_rows
            return attend_block(
                current,
                query_heads,
                query_frames,
                query_clips,
                piece_keys,
                piece_values,
                numbers,
                clip_lookup(numbers, table),
                "far",
            )

        def keep_state(current):
            return current

        state = lax.cond(useful, attend_here, keep_state, state)
        return (state, None)

    inner, _ = lax.scan(one_block, inner, jnp.arange(rows_here // block, dtype=jnp.int32))
    carried = inner
    top_final, totals, summed = carried
    result = summed / jnp.transpose(totals)[:, :, None]
    return result.reshape(fr_dev, tok, width).astype(jnp.bfloat16)


def solution(mesh):
    placed = (
        P(("dp", "tm"), None, None),
        P(("dp", "tm"), None, None),
        P(("dp", "tm"), None, None),
        P(("dp", "tm")),
    )
    return jax.shard_map(
        on_device,
        mesh=mesh,
        in_specs=placed,
        out_specs=P(("dp", "tm"), None, None),
        check_vma=False,
    )
```

profile of v0, /device:TPU:1, one launch (start us, length us, event | category | flops | bytes accessed | tf_op | source)
XLA Modules:
  0.0 190.6 jit_solution(14980208690735506288)
XLA Ops:
  6.5 1.3 reshape.309
  7.9 0.2 reduce_sum.88
  8.1 0.6 convert_element_type.78
  8.7 0.0 all-gather.3.cloned.1.call-update
  8.8 0.0 all-gather.5.cloned.1.call-start
  8.8 0.5 reshape.307
  9.3 0.7 reduce_sum.85
  10.1 0.5 reshape.308
  10.6 0.7 reduce_sum.86
  11.3 0.6 constant_dynamic-update-slice_fusion.1
  12.0 0.6 constant_dynamic-update-slice_fusion
  12.6 4.6 %collective-permute-start = (bf16[2,32,1536]{2,1,0:T(8,128)(2,1)}, bf16[2,32,1536]{2,1,0:T(8,128)(2,1)}, u32[]{:S(2)}, u32[]{:S(2)}) collective-permute-start(bf16[2,32,1536]{2,1,0:T(8,128)(2,1)} %constant_dynamic-update-slice_fusion), channel_id=1, source_target_pairs={{0,1},{1,2},{2,3},{3,4},{4,5},{5,6},{6,7},{7,8},{8,9},{9,10},{10,1... | collective-permute-start | bytes 589832 | tf_op jit(solution)/shard_map/ppermute | solution.py:14
  17.2 0.2 reshape.310
  17.5 0.0 copy-start.16
  17.5 0.0 copy-start.11
  17.5 0.2 reduce_sum.89
  17.8 0.6 convert_element_type.80
  18.4 0.0 all-gather.5.cloned.1.call-update
  18.4 1.3 reshape_reshape.6
  19.8 0.4 reshape_reshape.7
  20.2 0.1 broadcast_in_dim.137
  20.3 0.1 reshape.305
  20.4 0.1 broadcast_in_dim.138
  20.5 0.1 reshape.306
  20.5 0.6 dynamic-slice
  21.8 0.2 dynamic-update-slice
  22.0 19.9 %all-reduce = s32[128]{0:T(128)S(1)} all-reduce(s32[128]{0:T(128)S(1)} %dynamic-update-slice), channel_id=1, replica_groups=mesh['dp'=4,'tm'=64] {'tm'}, use_global_device_ids=true, to_apply=%add | all-reduce | flops 128 | bytes 1024
  41.9 0.6 copy-done.17
  42.5 0.1 broadcast_in_dim.131
  42.5 0.1 sub.135
  42.6 0.1 broadcast_in_dim.136
  42.7 0.7 eq.80
  43.4 0.4 reshape.304
  43.8 0.5 copy.21
  44.3 0.1 pad_add_fusion
  44.4 0.2 select_reduce_fusion.1
  44.6 0.1 subtract_compare_fusion.1
  44.7 2.1 %fusion.51 = (f32[24,128]{1,0:T(8,128)}, f32[24,128,128]{1,2,0:T(8,128)S(1)}) fusion(bf16[128,24,64]{0,2,1:T(8,128)(2,1)S(1)} %copy.21, bf16[128,24,64]{2,1,0:T(8,128)(2,1)} %reshape_reshape.6, pred[128,128]{0,1:T(8,128)(4,1)S(1)} %subtract_compare_fusion.1), kind=kOutput, calls=%fused_computation.87 | convolution fusion | flops 51508224 | bytes 2387968 | tf_op jit(solution)/shard_map/qhe,khe->hqk/dot_general | solution.py:51
  46.8 1.4 fusion.44
  48.2 1.8 pad_maximum_fusion
  50.0 1.2 reshape_squeeze.6
  51.2 1.8 copy.27
  53.0 1.3 fusion.52
  54.4 0.2 fusion.36
  54.5 0.3 fusion.28
  54.9 0.5 fusion.26
  55.4 0.5 copy-done.5
  55.9 0.3 fusion.23
  56.1 35.2 %all-gather.3.cloned.1.call-done = bf16[512,1536]{1,0:T(8,128)(2,1)} async-done(((bf16[8,1536]{1,0:T(8,128)(2,1)}), bf16[512,1536]{1,0:T(8,128)(2,1)}) %all-gather.3.cloned.1.call-update) | async-done | bytes 1572880 | tf_op jit(solution)/shard_map/all_gather | solution.py:133
  91.4 77.4 %all-gather.5.cloned.1.call-done = bf16[512,1536]{1,0:T(8,128)(2,1)} async-done(((bf16[8,1536]{1,0:T(8,128)(2,1)}), bf16[512,1536]{1,0:T(8,128)(2,1)}) %all-gather.5.cloned.1.call-update) | async-done | bytes 1572880 | tf_op jit(solution)/shard_map/all_gather | solution.py:134
  168.7 12.9 %conditional.1 = ((f32[24,128]{1,0:T(8,128)S(1)}, f32[128,24,64]{0,2,1:T(8,128)S(1)})) conditional(s32[]{:T(128)} %convert_element_type.68, (f32[24,128]{1,0:T(8,128)S(1)}, f32[128,24,64]{0,2,1:T(8,128)S(1)}) %tuple.19, (s32[2,64]{1,0:T(2,128)S(1)}, s32[128]{0:T(128)S(1)}, s32[2,64]{1,0:T(2,128)S(1)}, bf16[512,1536]{1,0:T(8,128)(2,1)}, ...), branch_computations={%region_9.10_spmd, %region_10.14_spmd} | conditional | flops 423965824 | bytes 62188112 | solution.py:163
  168.8 0.2 select_reduce_fusion
  169.0 0.1 eq.62
  169.1 0.1 sub.106
  169.2 0.1 fusion.14
  169.3 1.7 copy.28
  171.0 1.1 fusion
  172.2 2.0 %fusion.2 = f32[24,128]{1,0:T(8,128)S(1)} fusion(f32[24,128,512]{2,1,0:T(8,128)S(1)} %get-tuple-element.114, f32[24,128]{1,0:T(8,128)S(1)} %get-tuple-element.112, pred[128,512]{1,0:T(8,128)(4,1)S(1)} %fusion.14), kind=kLoop, calls=%fused_computation.4 | loop fusion | flops 7861248 | bytes 6381568 | tf_op jit(solution)/shard_map/while/body/eval_jaxpr/cond/branch_1_fun/reduce_sum | solution.py:66
  174.2 0.6 copy-done
  174.9 1.6 copy.30
  176.5 5.1 %fusion.9 = f32[128,24,64]{0,2,1:T(8,128)S(1)} fusion(bf16[512,24,64]{0,2,1:T(8,128)(2,1)} %bitcast.42, f32[24,128,512]{2,1,0:T(8,128)} %copy-done, f32[24,128]{1,0:T(8,128)S(1)} %get-tuple-element.112, pred[128,512]{1,0:T(8,128)(4,1)S(1)} %fusion.14, f32[128,24,64]{0,2,1:T(8,128)S(1)} %get-tuple-element.87, f32[128,24]{0,1:T(8,128)S(1)} %get-tuple-element.111), kind=kOutput, calls=%fused_computation.8 | convolution fusion | flops 209584128 | bytes 9527296 | tf_op jit(solution)/shard_map/while/body/eval_jaxpr/cond/branch_1_fun/hqk,khe->qhe/dot_general | solution.py:67
  181.6 0.1 divide_convert_fusion
  181.7 0.3 reshape.316
  182.1 1.7 copy.33
  (54 shorter events, 0.4 us)
Async XLA Ops:
  6.5 2.3 %copy-start.1 = (bf16[2,64,1536]{2,1,0:T(8,128)(2,1)S(1)}, bf16[2,64,1536]{2,1,0:T(8,128)(2,1)}, u32[]{:S(2)}) copy-start(bf16[2,64,1536]{2,1,0:T(8,128)(2,1)} %param.7) | copy-start | bytes 1179652
  6.5 84.8 %all-gather.3.cloned.1.call-start = ((), (), s32[]{:S(2)}) async-start(), calls=%async_computation | async-start | bytes 1597440 | tf_op jit(solution)/shard_map/all_gather | solution.py:133
  8.1 2.0 %copy-start.2 = (bf16[2,64,1536]{2,1,0:T(8,128)(2,1)S(1)}, bf16[2,64,1536]{2,1,0:T(8,128)(2,1)}, u32[]{:S(2)}) copy-start(bf16[2,64,1536]{2,1,0:T(8,128)(2,1)} %param.8) | copy-start | bytes 1179652
  8.8 159.9 %all-gather.5.cloned.1.call-start = ((), (), s32[]{:S(2)}) async-start(), calls=%async_computation.1 | async-start | bytes 1597440 | tf_op jit(solution)/shard_map/all_gather | solution.py:134
  12.6 35.6 %collective-permute-start = (bf16[2,32,1536]{2,1,0:T(8,128)(2,1)}, bf16[2,32,1536]{2,1,0:T(8,128)(2,1)}, u32[]{:S(2)}, u32[]{:S(2)}) collective-permute-start(bf16[2,32,1536]{2,1,0:T(8,128)(2,1)} %constant_dynamic-update-slice_fusion), channel_id=1, source_target_pairs={{0,1},{1,2},{2,3},{3,4},{4,5},{5,6},{6,7},{7,8},{8,9},{9,10},{10,1... | collective-permute-start | bytes 589832 | tf_op jit(solution)/shard_map/ppermute | solution.py:14
  17.5 3.1 %copy-start.16 = (u32[256]{0:T(256)S(1)}, u32[256]{0:T(256)}, u32[]{:S(2)}) copy-start(u32[256]{0:T(256)} %constant.168) | copy-start | bytes 3076
  17.5 4.3 %copy-start.11 = (s32[2]{0:T(128)S(1)}, s32[2]{0:T(128)}, u32[]{:S(2)}) copy-start(s32[2]{0:T(128)} %param.9) | copy-start | bytes 28
  17.5 25.9 %copy-start.6 = (bf16[2,64,1536]{2,1,0:T(8,128)(2,1)S(1)}, bf16[2,64,1536]{2,1,0:T(8,128)(2,1)}, u32[]{:S(2)}) copy-start(bf16[2,64,1536]{2,1,0:T(8,128)(2,1)} %param.6) | copy-start | bytes 1179652
  41.9 0.6 copy-start.17
  42.5 2.1 %copy-start.12 = (s32[2,64]{1,0:T(2,128)}, s32[2,64]{1,0:T(2,128)S(1)}, u32[]{:S(2)}) copy-start(s32[2,64]{1,0:T(2,128)S(1)} %broadcast_in_dim.131) | copy-start | bytes 1540
  42.6 2.0 %copy-start.9 = (s32[128]{0:T(128)}, s32[128]{0:T(128)S(1)}, u32[]{:S(2)}) copy-start(s32[128]{0:T(128)S(1)} %sub.135) | copy-start | bytes 1540
  42.7 1.9 %copy-start.14 = (s32[2,64]{1,0:T(2,128)}, s32[2,64]{1,0:T(2,128)S(1)}, u32[]{:S(2)}) copy-start(s32[2,64]{1,0:T(2,128)S(1)} %broadcast_in_dim.136) | copy-start | bytes 1540
  44.3 5.7 %copy-start.4 = (bf16[128,24,64]{0,2,1:T(8,128)(2,1)}, bf16[128,24,64]{0,2,1:T(8,128)(2,1)S(1)}, u32[]{:S(2)}) copy-start(bf16[128,24,64]{0,2,1:T(8,128)(2,1)S(1)} %copy.21) | copy-start | bytes 1179652
  44.7 2.1 %copy-start.10 = (s32[128]{0:T(128)S(1)}, s32[128]{0:T(128)}, u32[]{:S(2)}) copy-start(s32[128]{0:T(128)} %copy-done.9) | copy-start | bytes 1540
  53.0 1.3 copy-start.8
  53.0 1.3 copy-start.7
  54.9 1.0 copy-start.5
  55.3 113.4 %copy-start.13 = (s32[2,64]{1,0:T(2,128)S(1)}, s32[2,64]{1,0:T(2,128)}, u32[]{:S(2)}) copy-start(s32[2,64]{1,0:T(2,128)} %copy-done.12) | copy-start | bytes 1540
  55.3 113.4 %copy-start.15 = (s32[2,64]{1,0:T(2,128)S(1)}, s32[2,64]{1,0:T(2,128)}, u32[]{:S(2)}) copy-start(s32[2,64]{1,0:T(2,128)} %copy-done.14) | copy-start | bytes 1540
  55.3 113.4 %copy-start.18 = (s32[128]{0:T(128)S(1)}, s32[128]{0:T(128)}, u32[]{:S(2)}) copy-start(s32[128]{0:T(128)} %copy-done.17) | copy-start | bytes 1540
  172.2 2.7 %copy-start = (f32[24,128,512]{2,1,0:T(8,128)}, f32[24,128,512]{2,1,0:T(8,128)S(1)}, u32[]{:S(2)}) copy-start(f32[24,128,512]{2,1,0:T(8,128)S(1)} %get-tuple-element.114) | copy-start | bytes 18874372 | tf_op jit(solution)/shard_map/while/body/eval_jaxpr/cond
  172.2 2.7 %copy-start.3 = (bf16[512,1536]{1,0:T(8,128)(2,1)S(1)}, bf16[512,1536]{1,0:T(8,128)(2,1)}, u32[]{:S(2)}) copy-start(bf16[512,1536]{1,0:T(8,128)(2,1)} %get-tuple-element.110) | copy-start | bytes 4718596 | tf_op jit(solution)/shard_map/while/body/eval_jaxpr/cond
Sparse Core Ops, SparseCore 0:
  10.1 81.1 all-gather.2
  94.1 74.5 all-gather.4
where the time goes:
time: 191 us
  waiting for transfers between devices  113 us (59%)
  local copies, waits for them, and re-layouts  20.1 us (11%)
  blocking collectives  19.9 us (10%)
  between operations  14.4 us (8%)
  matrix products  10.4 us (5%)
  other arithmetic  8.43 us (4%)
  starting transfers between devices  4.63 us (2%)
    all_gather x1, waiting for transfers between devices, on_device(): piece_values = lax.all_gather(far_values, 'tm', axis=0, tiled=True)  77.4 us
    all_gather x1, waiting for transfers between devices, on_device(): piece_keys = lax.all_gather(far_keys, 'tm', axis=0, tiled=True)  35.2 us
    unnamed x1, blocking collectives  19.9 us
    dot_general x3, matrix products, attend_block(): jnp.einsum('hqk,khe->qhe', weights.astype(jnp.bfloat16), value_heads, pre...  5.84 us
    ppermute x1, starting transfers between devices, passed_along(): lax.ppermute(value, axis, [(source, source + steps) for source in range(f...  4.58 us
    dot_general x3, matrix products, attend_block(): jnp.einsum('qhe,khe->hqk', query_heads, key_heads, preferred_element_type...  4.53 us
  transfers between devices with their start and end apart: 3, of which 2 were waited for; matrix products, arithmetic and copies ran while one was open for 11% of the time, Pallas kernels for 0%

commit v1 on v0

v1 whole, which is shorter than its diff:
```python
import functools

import jax
import jax.numpy as jnp
from jax import lax
from jax.experimental import pallas as pl
from jax.experimental.pallas import tpu as pltpu
from jax.sharding import PartitionSpec as P

HEAD_DIM = 64
SIDE = 8
TOK = 64
NZ, NY, NC = 8, 4, 2
FPC = 4
HALF = 768
PAIRS = HALF // 128
ROWS = FPC * TOK
LANES = 2 * ROWS
FAR = 4
BLK = FPC * FAR
LEVELS = 4
MIXED = LEVELS * NY
OWN = MIXED + NY
SLOTS = OWN + 1
NKF = SLOTS * BLK
NEAR_ROWS = 16
NKN = 5 * NEAR_ROWS
FLAT = (LEVELS + 2) * NY * FPC
BASE = FLAT - NY * FPC
NEG = -1e30
MESH = pl.DeviceIdType.MESH


def iota(shape, dim):
    return lax.broadcasted_iota(jnp.int32, shape, dim)


def remote(src, dst, ss, rs, to):
    return pltpu.make_async_remote_copy(
        src_ref=src, dst_ref=dst, send_sem=ss, recv_sem=rs, device_id={"tm": to}, device_id_type=MESH
    )


def nt(a, b):
    return lax.dot_general(a, b, (((1,), (1,)), ((), ())), preferred_element_type=jnp.float32)


def tn(a, b):
    return lax.dot_general(a, b, (((0,), (0,)), ((), ())), preferred_element_type=jnp.float32)


def kernel(
    q_hbm, k_hbm, v_hbm, clip_ref, out_hbm,
    qb, kb, vb, far, near, qm, clips, bias_far, bias_near, acc, tops, sums, ob,
    in_sem, sib_ss, sib_rs, z_ss, z_rs, y_ss, y_rs, near_ss, near_rs, cy_ss, cy_rs, cz_ss, cz_rs, o_ss, o_rs, o_ls,
):
    d = lax.axis_index("tm")
    z, y, c = d // (NY * NC), lax.rem(d // NC, NY), lax.rem(d, NC)
    chip = d // NC

    def dev(zz, yy, cc):
        return zz * (NY * NC) + yy * NC + cc

    sibling = dev(z, y, 1 - c)

    far[...] = jnp.zeros_like(far)
    near[:, : 2 * NEAR_ROWS] = jnp.zeros((2, 2 * NEAR_ROWS, HALF), jnp.bfloat16)
    clips[...] = jnp.zeros_like(clips)

    barrier = pltpu.get_barrier_semaphore()

    def greet(to):
        pl.semaphore_signal(barrier, inc=1, device_id={"tm": to}, device_id_type=MESH)

    for yy in range(1, NY):
        for cc in range(NC):
            greet(dev(z, lax.rem(y + yy, NY), cc))
    greet(sibling)
    for k in range(1, LEVELS + 2):
        @pl.when(z >= k)
        def _():
            greet(dev(z - k, y, c))

    @pl.when((y == 0) & (z > 0))
    def _():
        greet(dev(z - 1, NY - 1, c))

    lo = pl.multiple_of(c * HALF, 128)
    hi = pl.multiple_of((1 - c) * HALF, 128)
    mine = pl.ds(2 * c, 2)
    local = []
    for n, (src, dst) in enumerate(((k_hbm, kb), (v_hbm, vb), (q_hbm, qb))):
        cp = pltpu.make_async_copy(src.at[:, :, pl.ds(lo, HALF)], dst.at[mine], in_sem.at[n])
        cp.start()
        local.append(cp)

    up = jnp.minimum(NZ - 1 - z, LEVELS + 1)
    next_near = jnp.where((y == NY - 1) & (z < NZ - 1), 1, 0)
    pl.semaphore_wait(barrier, (NY - 1) * NC + 1 + up + next_near)

    halves = []
    for n, (src, dst) in enumerate(((k_hbm, kb), (v_hbm, vb), (q_hbm, qb))):
        cp = remote(src.at[:, :, pl.ds(hi, HALF)], dst.at[mine], sib_ss.at[n], sib_rs.at[n], sibling)
        cp.start()
        halves.append(cp)

    def wait_half(n):
        local[n].wait()
        other = (kb, vb, qb)[n].at[pl.ds(2 * (1 - c), 2)]
        remote(other, other, sib_ss.at[n], sib_rs.at[n], sibling).wait_recv()

    row = y * NC + c
    clips[LEVELS + 1, row] = jnp.concatenate(
        [jnp.full((1, 128), clip_ref[n].astype(jnp.float32)) for n in range(2)], axis=0
    )
    level_sends = []
    for n in range(1, NY * NC):
        to = lax.rem(row + n, NY * NC)
        ref = clips.at[LEVELS + 1, row]
        cp = remote(ref, ref, cy_ss.at[n], cy_rs.at[n], z * (NY * NC) + to)
        cp.start()
        level_sends.append(cp)

    r = iota((NEAR_ROWS * FPC + BLK, ROWS), 0)
    t = iota((NEAR_ROWS * FPC + BLK, ROWS), 1)
    frame, token = t // TOK, lax.rem(t, TOK)
    line, place = token // SIDE, lax.rem(token, SIDE)
    near_row = frame * NEAR_ROWS + (line // 2) * 4 + place // 2
    far_row = NEAR_ROWS * FPC + frame * FAR + (line // 4) * 2 + place // 4
    pool = jnp.where(r == near_row, 0.25, jnp.where(r == far_row, 0.0625, 0.0)).astype(jnp.bfloat16)
    for n, full in enumerate((kb, vb)):
        wait_half(n)
        pooled = jnp.dot(pool, full[...].reshape(ROWS, HALF), preferred_element_type=jnp.float32)
        pooled = pooled.astype(jnp.bfloat16)
        near[n, 2 * NEAR_ROWS :] = pooled[: NEAR_ROWS * FPC]
        far[n, OWN] = pooled[NEAR_ROWS * FPC :]

    def slot(k, col):
        return (k - 1) * NY + col

    for k in range(1, LEVELS + 2):
        @pl.when(z + k < NZ)
        def _():
            remote(far.at[:, OWN], far.at[:, slot(k, y)], z_ss.at[k], z_rs.at[k], dev(z + k, y, c)).start()

    def mixed(delta, src):
        return remote(
            far.at[:, src], far.at[:, MIXED + y], y_ss.at[LEVELS + 1, delta], y_rs.at[LEVELS + 1, delta],
            dev(z, lax.rem(y + delta, NY), c),
        )

    for delta in range(1, NY):
        @pl.when(y + delta < NY)
        def _():
            mixed(delta, OWN).start()

    near_out = remote(
        near.at[:, pl.ds(4 * NEAR_ROWS, 2 * NEAR_ROWS)], near.at[:, pl.ds(0, 2 * NEAR_ROWS)],
        near_ss.at[0], near_rs.at[0], jnp.minimum((chip + 1) * NC + c, NZ * NY * NC - 1),
    )

    @pl.when(chip < NZ * NY - 1)
    def _():
        near_out.start()

    for n in range(1, NY * NC):
        ref = clips.at[LEVELS + 1, lax.rem(row + NY * NC - n, NY * NC)]
        remote(ref, ref, cy_ss.at[n], cy_rs.at[n], d).wait_recv()
    for k in range(1, LEVELS + 2):
        @pl.when(z + k < NZ)
        def _():
            remote(
                clips.at[LEVELS + 1], clips.at[LEVELS + 1 - k], cz_ss.at[k], cz_rs.at[k], dev(z + k, y, c)
            ).start()

    wait_half(2)
    even = iota((TOK, 128), 1) < HEAD_DIM
    for p in range(PAIRS):
        for i in range(FPC):
            part = qb[i, :, p * 128 : (p + 1) * 128] * jnp.bfloat16(HEAD_DIM ** -0.5)
            qm[p, i * 128 : i * 128 + TOK] = jnp.where(even, part, jnp.zeros_like(part))
            qm[p, i * 128 + TOK : (i + 1) * 128] = jnp.where(even, jnp.zeros_like(part), part)

    def spread(k, delta):
        ref = far.at[:, slot(k, y)]
        return remote(ref, ref, y_ss.at[k, delta], y_rs.at[k, delta], dev(z, lax.rem(y + delta, NY), c))

    for k in range(1, LEVELS + 1):
        @pl.when(z >= k)
        def _():
            ref = far.at[:, slot(k, y)]
            remote(ref, ref, z_ss.at[k], z_rs.at[k], d).wait_recv()
            for delta in range(1, NY):
                spread(k, delta).start()

    @pl.when(z >= LEVELS + 1)
    def _():
        ref = far.at[:, MIXED + y]
        remote(ref, ref, z_ss.at[LEVELS + 1], z_rs.at[LEVELS + 1], d).wait_recv()
        for delta in range(1, NY):
            @pl.when(y + delta >= NY)
            def _():
                mixed(delta, MIXED + y).start()

    for k in range(1, LEVELS + 2):
        @pl.when(z >= k)
        def _():
            ref = clips.at[LEVELS + 1 - k]
            remote(ref, ref, cz_ss.at[k], cz_rs.at[k], d).wait_recv()
    flat_clips = clips[...].reshape(FLAT, 128)
    own_first = BASE + 4 * y
    lane = iota((1, 128), 1)
    query_clip = []
    for i in range(FPC):
        at = iota((FLAT, 128), 0) == own_first + i
        query_clip.append(jnp.sum(jnp.where(at, flat_clips, 0.0), axis=0, keepdims=True))
    flat_bf = flat_clips.astype(jnp.bfloat16)

    def key_clips(numbers, rows):
        pick = (numbers == iota((rows, FLAT), 1)).astype(jnp.float32).astype(jnp.bfloat16)
        return jnp.dot(pick, flat_bf, preferred_element_type=jnp.float32)

    def far_numbers(shape):
        n = iota(shape, 0)
        at, frame = n // BLK, lax.rem(n, BLK) // FAR
        col = lax.rem(at, NY)
        regular = (LEVELS - at // NY) * (NY * FPC) + col * FPC + frame
        shared = jnp.where(col < y, BASE, 0) + col * FPC + frame
        return jnp.where(at < MIXED, regular, jnp.where(at < OWN, shared, own_first + frame))

    def near_numbers(shape):
        return own_first - 2 + iota(shape, 0) // NEAR_ROWS

    floor = (LEVELS + 1 - z) * (NY * FPC)
    for numbers, rows, bias in ((near_numbers, NKN, bias_near), (far_numbers, NKF, bias_far)):
        clip_of = key_clips(numbers((rows, FLAT)), rows)
        number = numbers((rows, 128))
        for i in range(FPC):
            distance = own_first + i - number
            seen = (distance >= 1) & (distance <= 2) if rows == NKN else distance > 2
            ok = seen & (number >= floor) & (clip_of == query_clip[i])
            bias[:, i * 128 : (i + 1) * 128] = jnp.where(ok, 0.0, NEG)

    @pl.when(chip > 0)
    def _():
        ref = near.at[:, pl.ds(0, 2 * NEAR_ROWS)]
        remote(ref, ref, near_ss.at[0], near_rs.at[0], d).wait_recv()

    first_head = lax.rem(iota((1, LANES), 1), 128) < TOK

    def pick_head(both):
        return jnp.where(first_head, both[:HEAD_DIM], both[HEAD_DIM:])

    def cols(p):
        return pl.ds(pl.multiple_of(p * 128, 128), 128)

    def close(p, carry):
        qp = qm[p]
        own = jnp.concatenate(
            [nt(kb[i, :, cols(p)], qp[i * 128 : (i + 1) * 128]) for i in range(FPC)], axis=1
        )
        by = nt(near[0, :NKN, cols(p)], qp) + bias_near[...]
        top = jnp.maximum(jnp.max(own, axis=0, keepdims=True), jnp.max(by, axis=0, keepdims=True))
        own = jnp.exp(own - top)
        by = jnp.exp(by - top)
        tops[p] = top
        sums[p] = jnp.sum(own, axis=0, keepdims=True) + jnp.sum(by, axis=0, keepdims=True)
        own = own.astype(jnp.bfloat16)
        mixed_own = jnp.concatenate(
            [tn(vb[i, :, cols(p)], own[:, i * 128 : (i + 1) * 128]) for i in range(FPC)], axis=1
        )
        acc[p] = pick_head(mixed_own + tn(near[1, :NKN, cols(p)], by.astype(jnp.bfloat16)))
        return carry

    lax.fori_loop(0, PAIRS, close, 0)

    for k in range(1, LEVELS + 1):
        @pl.when(z >= k)
        def _():
            for delta in range(1, NY):
                ref = far.at[:, slot(k, lax.rem(y + NY - delta, NY))]
                remote(ref, ref, y_ss.at[k, delta], y_rs.at[k, delta], d).wait_recv()
    for delta in range(1, NY):
        @pl.when((y >= delta) | (z >= LEVELS + 1))
        def _():
            ref = far.at[:, MIXED + lax.rem(y + NY - delta, NY)]
            remote(ref, ref, y_ss.at[LEVELS + 1, delta], y_rs.at[LEVELS + 1, delta], d).wait_recv()

    theirs = pl.ds(2 * (1 - c), 2)

    def out_local(p):
        return pltpu.make_async_copy(
            ob.at[p, mine], out_hbm.at[:, :, pl.ds(pl.multiple_of(lo + p * 128, 128), 128)], o_ls.at[p]
        )

    def out_remote(p):
        return remote(
            ob.at[p, theirs], out_hbm.at[:, :, pl.ds(pl.multiple_of(lo + p * 128, 128), 128)],
            o_ss.at[p], o_rs.at[p], sibling,
        )

    def history(p, carry):
        scores = nt(far[0, :, :, cols(p)].reshape(NKF, 128), qm[p]) + bias_far[...]
        old = tops[p]
        top = jnp.maximum(old, jnp.max(scores, axis=0, keepdims=True))
        weights = jnp.exp(scores - top)
        factor = jnp.exp(old - top)
        total = sums[p] * factor + jnp.sum(weights, axis=0, keepdims=True)
        both = tn(far[1, :, :, cols(p)].reshape(NKF, 128), weights.astype(jnp.bfloat16))
        result = (acc[p] * factor + pick_head(both)) / total
        for i in range(FPC):
            turned = result[:, i * 128 : (i + 1) * 128].T
            ob[p, i] = jnp.concatenate([turned[:TOK], turned[TOK:]], axis=1).astype(jnp.bfloat16)
        out_local(p).start()
        out_remote(p).start()
        return carry

    lax.fori_loop(0, PAIRS, history, 0)

    for p in range(PAIRS):
        out_local(p).wait()
        out_remote(p).wait_send()
        ref = out_hbm.at[:, :, pl.ds(pl.multiple_of(hi + p * 128, 128), 128)]
        remote(ref, ref, o_ss.at[p], o_rs.at[p], sibling).wait_recv()
    for n in range(3):
        halves[n].wait_send()
    for cp in level_sends:
        cp.wait_send()
    for k in range(1, LEVELS + 2):
        @pl.when(z + k < NZ)
        def _():
            remote(far.at[:, OWN], far.at[:, slot(k, y)], z_ss.at[k], z_rs.at[k], d).wait_send()
            remote(clips.at[LEVELS + 1], clips.at[LEVELS + 1 - k], cz_ss.at[k], cz_rs.at[k], d).wait_send()

    @pl.when(chip < NZ * NY - 1)
    def _():
        near_out.wait_send()

    for delta in range(1, NY):
        @pl.when((y + delta < NY) | (z >= LEVELS + 1))
        def _():
            mixed(delta, OWN).wait_send()
        for k in range(1, LEVELS + 1):
            @pl.when(z >= k)
            def _():
                spread(k, delta).wait_send()


def on_device(queries, key_states, value_states, clip_ids):
    bf, f32 = jnp.bfloat16, jnp.float32
    dma = pltpu.SemaphoreType.DMA
    anywhere = pl.BlockSpec(memory_space=pl.ANY)
    return pl.pallas_call(
        kernel,
        out_shape=jax.ShapeDtypeStruct(queries.shape, bf),
        in_specs=[anywhere, anywhere, anywhere, pl.BlockSpec(memory_space=pltpu.SMEM)],
        out_specs=anywhere,
        scratch_shapes=[
            pltpu.VMEM((FPC, TOK, HALF), bf),
            pltpu.VMEM((FPC, TOK, HALF), bf),
            pltpu.VMEM((FPC, TOK, HALF), bf),
            pltpu.VMEM((2, SLOTS, BLK, HALF), bf),
            pltpu.VMEM((2, 6 * NEAR_ROWS, HALF), bf),
            pltpu.VMEM((PAIRS, LANES, 128), bf),
            pltpu.VMEM((LEVELS + 2, NY * NC, 2, 128), f32),
            pltpu.VMEM((NKF, LANES), f32),
            pltpu.VMEM((NKN, LANES), f32),
            pltpu.VMEM((PAIRS, HEAD_DIM, LANES), f32),
            pltpu.VMEM((PAIRS, 1, LANES), f32),
            pltpu.VMEM((PAIRS, 1, LANES), f32),
            pltpu.VMEM((PAIRS, FPC, TOK, 128), bf),
            dma((3,)),
            dma((3,)), dma((3,)),
            dma((LEVELS + 2,)), dma((LEVELS + 2,)),
            dma((LEVELS + 2, NY)), dma((LEVELS + 2, NY)),
            dma((1,)), dma((1,)),
            dma((NY * NC,)), dma((NY * NC,)),
            dma((LEVELS + 2,)), dma((LEVELS + 2,)),
            dma((PAIRS,)), dma((PAIRS,)), dma((PAIRS,)),
        ],
        compiler_params=pltpu.CompilerParams(
            collective_id=0, has_side_effects=True, vmem_limit_bytes=40 << 20
        ),
        cost_estimate=pl.CostEstimate(flops=1 << 30, bytes_accessed=4 << 20, transcendentals=1 << 21),
    )(queries, key_states, value_states, clip_ids)


def solution(mesh):
    frames = P(("dp", "tm"), None, None)
    return jax.shard_map(
        on_device,
        mesh=mesh,
        in_specs=(frames, frames, frames, P(("dp", "tm"))),
        out_specs=frames,
        check_vma=False,
    )
```

time: 191 us -> 38 us (0.20)
  the two profiles are of different devices: /device:TPU:1 before, /device:TPU:163 now
where the time goes in v1:
time: 38 us; the launch traced here: 37.8 us
  Pallas kernels  33.4 us (88%)
  local copies, waits for them, and re-layouts  4.39 us (12%)
    pallas_call x1, Pallas kernels, on_device(): pl.pallas_call(kernel, out_shape=jax.ShapeDtypeStruct(queries.shape, bf),...  33.4 us
    unnamed x9, local copies, waits for them, and re-layouts  4.39 us

profile of v1, /device:TPU:163, one launch (start us, length us, event | category | flops | bytes accessed | tf_op | source)
XLA Modules:
  0.0 37.8 jit_solution(15431481410096306205)
XLA Ops:
  0.0 0.0 copy-start
  0.0 1.0 %copy-done = bf16[2,64,1536]{2,1,0:T(8,128)(2,1)S(1)} copy-done((bf16[2,64,1536]{2,1,0:T(8,128)(2,1)S(1)}, bf16[2,64,1536]{2,1,0:T(8,128)(2,1)}, u32[]{:S(2)}) %copy-start) | copy-done | bytes 393240
  1.0 0.0 copy-start.1
  1.0 1.0 %copy-done.1 = bf16[2,64,1536]{2,1,0:T(8,128)(2,1)S(1)} copy-done((bf16[2,64,1536]{2,1,0:T(8,128)(2,1)S(1)}, bf16[2,64,1536]{2,1,0:T(8,128)(2,1)}, u32[]{:S(2)}) %copy-start.1) | copy-done | bytes 393240
  2.0 0.0 copy-start.2
  2.0 1.0 %copy-done.2 = bf16[2,64,1536]{2,1,0:T(8,128)(2,1)S(1)} copy-done((bf16[2,64,1536]{2,1,0:T(8,128)(2,1)S(1)}, bf16[2,64,1536]{2,1,0:T(8,128)(2,1)}, u32[]{:S(2)}) %copy-start.2) | copy-done | bytes 393240
  3.0 0.0 copy-start.3
  3.0 0.7 %copy-done.3 = s32[2]{0:T(128)S(1)} copy-done((s32[2]{0:T(128)S(1)}, s32[2]{0:T(128)}, u32[]{:S(2)}) %copy-start.3) | copy-done | bytes 32
  3.6 33.4 %shard_map.46 = bf16[2,64,1536]{2,1,0:T(8,128)(2,1)S(1)} custom-call(bf16[2,64,1536]{2,1,0:T(8,128)(2,1)S(1)} %copy-done, bf16[2,64,1536]{2,1,0:T(8,128)(2,1)S(1)} %copy-done.1, bf16[2,64,1536]{2,1,0:T(8,128)(2,1)S(1)} %copy-done.2, s32[2]{0:T(128)S(1)} %copy-done.3), custom_call_target="tpu_custom_call" | custom-call | flops 1073741824 | bytes 4194304 | tf_op jit(solution)/shard_map/pallas_call | solution.py:353
  37.0 0.7 %copy.6 = bf16[2,64,1536]{2,1,0:T(8,128)(2,1)} copy(bf16[2,64,1536]{2,1,0:T(8,128)(2,1)S(1)} %shard_map.46) | data formatting | bytes 786432
Async XLA Ops:
  0.0 1.0 %copy-start = (bf16[2,64,1536]{2,1,0:T(8,128)(2,1)S(1)}, bf16[2,64,1536]{2,1,0:T(8,128)(2,1)}, u32[]{:S(2)}) copy-start(bf16[2,64,1536]{2,1,0:T(8,128)(2,1)} %q_hbm.1) | copy-start | bytes 1179652
  1.0 1.0 %copy-start.1 = (bf16[2,64,1536]{2,1,0:T(8,128)(2,1)S(1)}, bf16[2,64,1536]{2,1,0:T(8,128)(2,1)}, u32[]{:S(2)}) copy-start(bf16[2,64,1536]{2,1,0:T(8,128)(2,1)} %k_hbm.1) | copy-start | bytes 1179652
  2.0 1.0 %copy-start.2 = (bf16[2,64,1536]{2,1,0:T(8,128)(2,1)S(1)}, bf16[2,64,1536]{2,1,0:T(8,128)(2,1)}, u32[]{:S(2)}) copy-start(bf16[2,64,1536]{2,1,0:T(8,128)(2,1)} %v_hbm.1) | copy-start | bytes 1179652
  3.0 0.7 %copy-start.3 = (s32[2]{0:T(128)S(1)}, s32[2]{0:T(128)}, u32[]{:S(2)}) copy-start(s32[2]{0:T(128)} %clip_ref.1) | copy-start | bytes 28

commit v2 on v1

--- a/solution.py
+++ b/solution.py
@@ -19,9 +19,12 @@
 FAR = 4
 BLK = FPC * FAR
 LEVELS = 4
-MIXED = LEVELS * NY
-OWN = MIXED + NY
-SLOTS = OWN + 1
+OWN = 0
+ORDER = (1, 2, 5, 3, 4)
+FIRST = {k: 1 + n * NY for n, k in enumerate(ORDER)}
+MIXED = FIRST[LEVELS + 1]
+SLOTS = 1 + 5 * NY
+EARLY = FIRST[3]
 NKF = SLOTS * BLK
 NEAR_ROWS = 16
 NKN = 5 * NEAR_ROWS
@@ -50,8 +53,8 @@
 
 
 def kernel(
-    q_hbm, k_hbm, v_hbm, clip_ref, out_hbm,
-    qb, kb, vb, far, near, qm, clips, bias_far, bias_near, acc, tops, sums, ob,
+    q_hbm, k_hbm, v_hbm, clip_hbm, out_hbm,
+    clip_ref, qb, kb, vb, far, near, qm, level_clips, clips, bias_far, bias_near, acc, tops, sums, ob,
     in_sem, sib_ss, sib_rs, z_ss, z_rs, y_ss, y_rs, near_ss, near_rs, cy_ss, cy_rs, cz_ss, cz_rs, o_ss, o_rs, o_ls,
 ):
     d = lax.axis_index("tm")
@@ -94,6 +97,9 @@
         cp.start()
         local.append(cp)
 
+    clip_copy = pltpu.make_async_copy(clip_hbm, clip_ref, in_sem.at[3])
+    clip_copy.start()
+
     up = jnp.minimum(NZ - 1 - z, LEVELS + 1)
     next_near = jnp.where((y == NY - 1) & (z < NZ - 1), 1, 0)
     pl.semaphore_wait(barrier, (NY - 1) * NC + 1 + up + next_near)
@@ -109,14 +115,16 @@
         other = (kb, vb, qb)[n].at[pl.ds(2 * (1 - c), 2)]
         remote(other, other, sib_ss.at[n], sib_rs.at[n], sibling).wait_recv()
 
+    clip_copy.wait()
     row = y * NC + c
-    clips[LEVELS + 1, row] = jnp.concatenate(
-        [jnp.full((1, 128), clip_ref[n].astype(jnp.float32)) for n in range(2)], axis=0
+    lane = iota((1, 128), 1)
+    level_clips[row] = sum(
+        jnp.where(lane == 2 * row + n, clip_ref[n].astype(jnp.float32), 0.0) for n in range(2)
     )
     level_sends = []
     for n in range(1, NY * NC):
         to = lax.rem(row + n, NY * NC)
-        ref = clips.at[LEVELS + 1, row]
+        ref = level_clips.at[row]
         cp = remote(ref, ref, cy_ss.at[n], cy_rs.at[n], z * (NY * NC) + to)
         cp.start()
         level_sends.append(cp)
@@ -136,12 +144,27 @@
         far[n, OWN] = pooled[NEAR_ROWS * FPC :]
 
     def slot(k, col):
-        return (k - 1) * NY + col
-
-    for k in range(1, LEVELS + 2):
+        return FIRST[k] + col
+
+    def rise(k):
+        return remote(far.at[:, OWN], far.at[:, slot(k, y)], z_ss.at[k], z_rs.at[k], dev(z + k, y, c))
+
+    def start_rise(k):
         @pl.when(z + k < NZ)
         def _():
-            remote(far.at[:, OWN], far.at[:, slot(k, y)], z_ss.at[k], z_rs.at[k], dev(z + k, y, c)).start()
+            rise(k).start()
+
+    def sent_rise(k):
+        @pl.when(z + k < NZ)
+        def _():
+            rise(k).wait_send()
+
+    for k in (1, 2, 5):
+        start_rise(k)
+
+    @pl.when(z == NZ - 1 - LEVELS)
+    def _():
+        rise(4).start()
 
     def mixed(delta, src):
         return remote(
@@ -149,7 +172,7 @@
             dev(z, lax.rem(y + delta, NY), c),
         )
 
-    for delta in range(1, NY):
+    for delta in (1, 3, 2):
         @pl.when(y + delta < NY)
         def _():
             mixed(delta, OWN).start()
@@ -164,8 +187,9 @@
         near_out.start()
 
     for n in range(1, NY * NC):
-        ref = clips.at[LEVELS + 1, lax.rem(row + NY * NC - n, NY * NC)]
+        ref = level_clips.at[lax.rem(row + NY * NC - n, NY * NC)]
         remote(ref, ref, cy_ss.at[n], cy_rs.at[n], d).wait_recv()
+    clips[LEVELS + 1] = jnp.sum(level_clips[...], axis=0)
     for k in range(1, LEVELS + 2):
         @pl.when(z + k < NZ)
         def _():
@@ -185,56 +209,78 @@
         ref = far.at[:, slot(k, y)]
         return remote(ref, ref, y_ss.at[k, delta], y_rs.at[k, delta], dev(z, lax.rem(y + delta, NY), c))
 
-    for k in range(1, LEVELS + 1):
+    def arrived(k):
+        ref = far.at[:, slot(k, y)]
+        remote(ref, ref, z_ss.at[k], z_rs.at[k], d).wait_recv()
+
+    def forward():
+        return remote(far.at[:, slot(2, y)], far.at[:, slot(3, y)], z_ss.at[3], z_rs.at[3], dev(z + 1, y, c))
+
+    def backward():
+        return remote(far.at[:, slot(5, y)], far.at[:, slot(4, y)], z_ss.at[4], z_rs.at[4], dev(z - 1, y, c))
+
+    def pass_on(k):
         @pl.when(z >= k)
         def _():
-            ref = far.at[:, slot(k, y)]
-            remote(ref, ref, z_ss.at[k], z_rs.at[k], d).wait_recv()
-            for delta in range(1, NY):
-                spread(k, delta).start()
-
-    @pl.when(z >= LEVELS + 1)
-    def _():
-        ref = far.at[:, MIXED + y]
-        remote(ref, ref, z_ss.at[LEVELS + 1], z_rs.at[LEVELS + 1], d).wait_recv()
-        for delta in range(1, NY):
-            @pl.when(y + delta >= NY)
-            def _():
-                mixed(delta, MIXED + y).start()
+            arrived(k)
+            if k == 2:
+                @pl.when(z < NZ - 1)
+                def _():
+                    forward().start()
+            if k == 5:
+                backward().start()
+            for delta in (1, 3, 2):
+                if k <= LEVELS:
+                    spread(k, delta).start()
+                else:
+                    @pl.when(y + delta >= NY)
+                    def _():
+                        mixed(delta, MIXED + y).start()
+
+    pass_on(1)
+    pass_on(2)
+    pass_on(5)
 
     for k in range(1, LEVELS + 2):
         @pl.when(z >= k)
         def _():
             ref = clips.at[LEVELS + 1 - k]
             remote(ref, ref, cz_ss.at[k], cz_rs.at[k], d).wait_recv()
-    flat_clips = clips[...].reshape(FLAT, 128)
+    table = clips[...].reshape(8, 128)
     own_first = BASE + 4 * y
-    lane = iota((1, 128), 1)
-    query_clip = []
-    for i in range(FPC):
-        at = iota((FLAT, 128), 0) == own_first + i
-        query_clip.append(jnp.sum(jnp.where(at, flat_clips, 0.0), axis=0, keepdims=True))
-    flat_bf = flat_clips.astype(jnp.bfloat16)
+    query_clip = [
+        jnp.sum(jnp.where(lane == 4 * y + i, table[LEVELS + 1 : LEVELS + 2], 0.0), axis=1, keepdims=True)
+        for i in range(FPC)
+    ]
+    table = table.astype(jnp.bfloat16)
+    ones = jnp.ones((128, 128), jnp.bfloat16)
 
     def key_clips(numbers, rows):
-        pick = (numbers == iota((rows, FLAT), 1)).astype(jnp.float32).astype(jnp.bfloat16)
-        return jnp.dot(pick, flat_bf, preferred_element_type=jnp.float32)
+        pick = (numbers // (NY * FPC))[:, :8] == iota((rows, 8), 1)
+        level = jnp.dot(pick.astype(jnp.float32).astype(jnp.bfloat16), table, preferred_element_type=jnp.float32)
+        one = jnp.where(lax.rem(numbers, NY * FPC) == iota((rows, 128), 1), level, 0.0)
+        return jnp.dot(one.astype(jnp.bfloat16), ones, preferred_element_type=jnp.float32)
 
     def far_numbers(shape):
         n = iota(shape, 0)
         at, frame = n // BLK, lax.rem(n, BLK) // FAR
-        col = lax.rem(at, NY)
-        regular = (LEVELS - at // NY) * (NY * FPC) + col * FPC + frame
+        step = at + NY - 1
+        col = lax.rem(step, NY)
+        level = functools.reduce(
+            lambda found, k: jnp.where(step // NY == ORDER.index(k) + 1, k, found), ORDER, 0
+        )
+        regular = (LEVELS + 1 - level) * (NY * FPC) + col * FPC + frame
         shared = jnp.where(col < y, BASE, 0) + col * FPC + frame
-        return jnp.where(at < MIXED, regular, jnp.where(at < OWN, shared, own_first + frame))
+        held = jnp.where((at >= MIXED) & (at < MIXED + NY), shared, regular)
+        return jnp.where(at == OWN, own_first + frame, held)
 
     def near_numbers(shape):
         return own_first - 2 + iota(shape, 0) // NEAR_ROWS
 
     floor = (LEVELS + 1 - z) * (NY * FPC)
     for numbers, rows, bias in ((near_numbers, NKN, bias_near), (far_numbers, NKF, bias_far)):
-        clip_of = key_clips(numbers((rows, FLAT)), rows)
         number = numbers((rows, 128))
+        clip_of = key_clips(number, rows)
         for i in range(FPC):
             distance = own_first + i - number
             seen = (distance >= 1) & (distance <= 2) if rows == NKN else distance > 2
@@ -272,14 +318,20 @@
         acc[p] = pick_head(mixed_own + tn(near[1, :NKN, cols(p)], by.astype(jnp.bfloat16)))
         return carry
 
-    lax.fori_loop(0, PAIRS, close, 0)
-
-    for k in range(1, LEVELS + 1):
+    lax.fori_loop(0, 4, close, 0)
+    pass_on(3)
+    pass_on(4)
+    lax.fori_loop(4, PAIRS, close, 0)
+
+    def level_here(k):
         @pl.when(z >= k)
         def _():
             for delta in range(1, NY):
                 ref = far.at[:, slot(k, lax.rem(y + NY - delta, NY))]
                 remote(ref, ref, y_ss.at[k, delta], y_rs.at[k, delta], d).wait_recv()
+
+    level_here(1)
+    level_here(2)
     for delta in range(1, NY):
         @pl.when((y >= delta) | (z >= LEVELS + 1))
         def _():
@@ -299,15 +351,25 @@
             o_ss.at[p], o_rs.at[p], sibling,
         )
 
-    def history(p, carry):
-        scores = nt(far[0, :, :, cols(p)].reshape(NKF, 128), qm[p]) + bias_far[...]
+    def history(p, first, last):
+        rows = (last - first) * BLK
+        keys = far[0, first:last, :, cols(p)].reshape(rows, 128)
+        scores = nt(keys, qm[p]) + bias_far[first * BLK : last * BLK]
         old = tops[p]
         top = jnp.maximum(old, jnp.max(scores, axis=0, keepdims=True))
         weights = jnp.exp(scores - top)
         factor = jnp.exp(old - top)
         total = sums[p] * factor + jnp.sum(weights, axis=0, keepdims=True)
-        both = tn(far[1, :, :, cols(p)].reshape(NKF, 128), weights.astype(jnp.bfloat16))
-        result = (acc[p] * factor + pick_head(both)) / total
+        both = tn(far[1, first:last, :, cols(p)].reshape(rows, 128), weights.astype(jnp.bfloat16))
+        return top, total, acc[p] * factor + pick_head(both)
+
+    def early(p, carry):
+        tops[p], sums[p], acc[p] = history(p, 0, EARLY)
+        return carry
+
+    def late(p, carry):
+        _, total, summed = history(p, EARLY, SLOTS)
+        result = summed / total
         for i in range(FPC):
             turned = result[:, i * 128 : (i + 1) * 128].T
             ob[p, i] = jnp.concatenate([turned[:TOK], turned[TOK:]], axis=1).astype(jnp.bfloat16)
@@ -315,7 +377,10 @@
         out_remote(p).start()
         return carry
 
-    lax.fori_loop(0, PAIRS, history, 0)
+    lax.fori_loop(0, PAIRS, early, 0)
+    level_here(3)
+    level_here(4)
+    lax.fori_loop(0, PAIRS, late, 0, unroll=True)
 
     for p in range(PAIRS):
         out_local(p).wait()
@@ -326,10 +391,25 @@
         halves[n].wait_send()
     for cp in level_sends:
         cp.wait_send()
+    for k in (1, 2, 5):
+        sent_rise(k)
+
+    @pl.when(z == NZ - 1 - LEVELS)
+    def _():
+        rise(4).wait_send()
+
+    @pl.when(z >= 5)
+    def _():
+        backward().wait_send()
+
+
+    @pl.when((z >= 2) & (z < NZ - 1))
+    def _():
+        forward().wait_send()
+
     for k in range(1, LEVELS + 2):
         @pl.when(z + k < NZ)
         def _():
-            remote(far.at[:, OWN], far.at[:, slot(k, y)], z_ss.at[k], z_rs.at[k], d).wait_send()
             remote(clips.at[LEVELS + 1], clips.at[LEVELS + 1 - k], cz_ss.at[k], cz_rs.at[k], d).wait_send()
 
     @pl.when(chip < NZ * NY - 1)
@@ -349,27 +429,29 @@
 def on_device(queries, key_states, value_states, clip_ids):
     bf, f32 = jnp.bfloat16, jnp.float32
     dma = pltpu.SemaphoreType.DMA
-    anywhere = pl.BlockSpec(memory_space=pl.ANY)
+    anywhere = pl.BlockSpec(memory_space=pltpu.HBM)
     return pl.pallas_call(
         kernel,
         out_shape=jax.ShapeDtypeStruct(queries.shape, bf),
-        in_specs=[anywhere, anywhere, anywhere, pl.BlockSpec(memory_space=pltpu.SMEM)],
+        in_specs=[anywhere] * 4,
         out_specs=anywhere,
         scratch_shapes=[
+            pltpu.SMEM((2,), jnp.int32),
             pltpu.VMEM((FPC, TOK, HALF), bf),
             pltpu.VMEM((FPC, TOK, HALF), bf),
             pltpu.VMEM((FPC, TOK, HALF), bf),
             pltpu.VMEM((2, SLOTS, BLK, HALF), bf),
             pltpu.VMEM((2, 6 * NEAR_ROWS, HALF), bf),
             pltpu.VMEM((PAIRS, LANES, 128), bf),
-            pltpu.VMEM((LEVELS + 2, NY * NC, 2, 128), f32),
+            pltpu.VMEM((NY * NC, 1, 128), f32),
+            pltpu.VMEM((8, 1, 128), f32),
             pltpu.VMEM((NKF, LANES), f32),
             pltpu.VMEM((NKN, LANES), f32),
             pltpu.VMEM((PAIRS, HEAD_DIM, LANES), f32),
             pltpu.VMEM((PAIRS, 1, LANES), f32),
             pltpu.VMEM((PAIRS, 1, LANES), f32),
             pltpu.VMEM((PAIRS, FPC, TOK, 128), bf),
-            dma((3,)),
+            dma((4,)),
             dma((3,)), dma((3,)),
             dma((LEVELS + 2,)), dma((LEVELS + 2,)),
             dma((LEVELS + 2, NY)), dma((LEVELS + 2, NY)),
@@ -379,7 +461,7 @@
             dma((PAIRS,)), dma((PAIRS,)), dma((PAIRS,)),
         ],
         compiler_params=pltpu.CompilerParams(
-            collective_id=0, has_side_effects=True, vmem_limit_bytes=40 << 20
+            collective_id=0, has_side_effects=True, vmem_limit_bytes=64 << 20
         ),
         cost_estimate=pl.CostEstimate(flops=1 << 30, bytes_accessed=4 << 20, transcendentals=1 << 21),
     )(queries, key_states, value_states, clip_ids)

time: 38 us -> 32.3 us (0.85)
  Pallas kernels: 33.4 us -> 30.4 us
  local copies, waits for them, and re-layouts: 4.39 us -> 1.77 us
    pallas_call x1, Pallas kernels: 33.4 us -> 30.4 us  [on_device(): pl.pallas_call(kernel, out_shape=jax.ShapeDtypeStruct(queries.shape, bf),...]
    unnamed x9 -> x1, local copies, waits for them, and re-layouts: 4.39 us -> 1.77 us
where the time goes in v2:
time: 32.3 us; the launch traced here: 32.2 us
  Pallas kernels  30.4 us (94%)
  local copies, waits for them, and re-layouts  1.77 us (5%)
    pallas_call x1, Pallas kernels, on_device(): pl.pallas_call(kernel, out_shape=jax.ShapeDtypeStruct(queries.shape, bf),...  30.4 us
    unnamed x1, local copies, waits for them, and re-layouts  1.77 us

profile of v2, /device:TPU:163, one launch (start us, length us, event | category | flops | bytes accessed | tf_op | source)
XLA Modules:
  0.0 32.2 jit_solution(11639948501555756070)
XLA Ops:
  0.0 30.4 %shard_map.46 = bf16[2,64,1536]{2,1,0:T(8,128)(2,1)} custom-call(bf16[2,64,1536]{2,1,0:T(8,128)(2,1)} %q_hbm.1, bf16[2,64,1536]{2,1,0:T(8,128)(2,1)} %k_hbm.1, bf16[2,64,1536]{2,1,0:T(8,128)(2,1)} %v_hbm.1, s32[2]{0:T(128)} %clip_hbm.1), custom_call_target="tpu_custom_call" | custom-call | flops 1073741824 | bytes 4194304 | tf_op jit(solution)/shard_map/pallas_call | solution.py:433
  30.4 1.8 %copy.6 = bf16[2,64,1536]{2,1,0:T(8,128)(2,1)} copy(bf16[2,64,1536]{2,1,0:T(8,128)(2,1)} %shard_map.46) | data formatting | bytes 786432

commit v3 on v2

v3 whole, which is shorter than its diff:
```python
import functools

import jax
import jax.numpy as jnp
from jax import lax
from jax.experimental import pallas as pl
from jax.experimental.pallas import tpu as pltpu
from jax.sharding import PartitionSpec as P

HEAD_DIM = 64
SIDE = 8
TOK = 64
NZ, NY, NC = 8, 4, 2
FPC = 4
HALF = 768
PAIRS = HALF // 128
ROWS = FPC * TOK
LANES = 2 * ROWS
FAR = 4
BLK = FPC * FAR
LEVELS = 4
OWN = 0
ORDER = (1, 2, 5, 3, 4)
FIRST = {k: 1 + n * NY for n, k in enumerate(ORDER)}
DIRECT = (1, 2, 5)
CHAINED = (2, 3)
MIXED = FIRST[LEVELS + 1]
SLOTS = 1 + 5 * NY
EARLY = FIRST[3]
NKF = SLOTS * BLK
NEAR_ROWS = 16
NKN = 5 * NEAR_ROWS
FLAT = (LEVELS + 2) * NY * FPC
BASE = FLAT - NY * FPC
NEG = -1e30
MESH = pl.DeviceIdType.MESH


def iota(shape, dim):
    return lax.broadcasted_iota(jnp.int32, shape, dim)


def remote(src, dst, ss, rs, to):
    return pltpu.make_async_remote_copy(
        src_ref=src, dst_ref=dst, send_sem=ss, recv_sem=rs, device_id={"tm": to}, device_id_type=MESH
    )


def nt(a, b):
    return lax.dot_general(a, b, (((1,), (1,)), ((), ())), preferred_element_type=jnp.float32)


def nn(a, b):
    return jnp.dot(a, b, preferred_element_type=jnp.float32)


def tn(a, b):
    return lax.dot_general(a, b, (((0,), (0,)), ((), ())), preferred_element_type=jnp.float32)


def kernel(
    q_hbm, k_hbm, v_hbm, clip_hbm, out_hbm,
    clip_ref, kf, vf, qb, kb, vb, pooled, far, near, qm, level_clips, clips, bias_far, bias_near, acc, tops, sums, ob,
    in_sem, sib_ss, sib_rs, own_ss, own_rs, z_ss, z_rs, m_ss, m_rs, y_ss, y_rs, x_ss,
    near_ss, near_rs, cy_ss, cy_rs, cz_ss, cz_rs, o_ss, o_rs, o_ls,
):
    d = lax.axis_index("tm")
    z, y, c = d // (NY * NC), lax.rem(d // NC, NY), lax.rem(d, NC)
    chip = d // NC

    def dev(zz, yy, cc):
        return zz * (NY * NC) + yy * NC + cc

    sibling = dev(z, y, 1 - c)

    lo = pl.multiple_of(c * HALF, 128)
    hi = pl.multiple_of((1 - c) * HALF, 128)
    mine = pl.ds(2 * c, 2)
    whole = []
    for n, (src, dst) in enumerate(((k_hbm, kf), (v_hbm, vf))):
        cp = pltpu.make_async_copy(src, dst, in_sem.at[n])
        cp.start()
        whole.append(cp)
    clip_copy = pltpu.make_async_copy(clip_hbm, clip_ref, in_sem.at[2])
    clip_copy.start()
    local = []
    for n, (src, dst) in enumerate(((k_hbm, kb), (v_hbm, vb), (q_hbm, qb))):
        cp = pltpu.make_async_copy(src.at[:, :, pl.ds(lo, HALF)], dst.at[mine], in_sem.at[3 + n])
        cp.start()
        local.append(cp)

    far[...] = jnp.zeros_like(far)
    near[:, : 2 * NEAR_ROWS] = jnp.zeros((2, 2 * NEAR_ROWS, HALF), jnp.bfloat16)
    clips[...] = jnp.zeros_like(clips)

    barrier = pltpu.get_barrier_semaphore()

    def greet(to):
        pl.semaphore_signal(barrier, inc=1, device_id={"tm": to}, device_id_type=MESH)

    for yy in range(1, NY):
        for cc in range(NC):
            greet(dev(z, lax.rem(y + yy, NY), cc))
    greet(sibling)
    for k in range(1, LEVELS + 2):
        @pl.when(z >= k)
        def _():
            greet(dev(z - k, y, c))
            if k in DIRECT:
                greet(dev(z - k, y, 1 - c))

    last_rise = NZ - 1 - LEVELS

    @pl.when(z == NZ - 1)
    def _():
        greet(dev(last_rise, y, 1 - c))

    @pl.when((y == 0) & (z > 0))
    def _():
        greet(dev(z - 1, NY - 1, c))

    def pool_matrix(rows, frames, side):
        r, t = iota((rows, frames * TOK), 0), iota((rows, frames * TOK), 1)
        frame, token = t // TOK, lax.rem(t, TOK)
        cells = SIDE // side
        at = frame * cells * cells + (token // SIDE // side) * cells + lax.rem(token, SIDE) // side
        return jnp.where(r == at, 1.0 / (side * side), 0.0).astype(jnp.bfloat16)

    far_pool = pool_matrix(2 * FAR, 2, 4)
    means = []
    for n, full in enumerate((kf, vf)):
        whole[n].wait()
        means.append(nn(far_pool, full[...].reshape(2 * TOK, 2 * HALF)))
    means = jnp.concatenate(means, axis=0).astype(jnp.bfloat16)
    for n in range(2):
        pooled[n] = means[:, n * HALF : (n + 1) * HALF]

    up = jnp.minimum(NZ - 1 - z, LEVELS + 1)
    crossing = sum(jnp.where(z + k < NZ, 1, 0) for k in DIRECT) + jnp.where(z == last_rise, 1, 0)
    next_near = jnp.where((y == NY - 1) & (z < NZ - 1), 1, 0)
    pl.semaphore_wait(barrier, (NY - 1) * NC + 1 + up + crossing + next_near)

    def slot(k, col):
        return FIRST[k] + col

    def rise(k, core):
        return remote(
            pooled.at[core], far.at[slot(k, y), c], z_ss.at[k, core], z_rs.at[k, c], dev(z + k, y, core)
        )

    def mixed(delta, core):
        return remote(
            pooled.at[core], far.at[MIXED + y, c], m_ss.at[delta, core], m_rs.at[delta, c],
            dev(z, lax.rem(y + delta, NY), core),
        )

    def each_rise(act):
        for k in DIRECT:
            @pl.when(z + k < NZ)
            def _():
                for core in range(NC):
                    act(rise(k, core))

        @pl.when(z == last_rise)
        def _():
            for core in range(NC):
                act(rise(LEVELS, core))

    def each_mixed(act):
        for delta in (1, 3, 2):
            @pl.when(y + delta < NY)
            def _():
                for core in range(NC):
                    act(mixed(delta, core))

    each_rise(lambda cp: cp.start())
    each_mixed(lambda cp: cp.start())
    across = remote(pooled.at[1 - c], far.at[OWN, c], own_ss.at[0], own_rs.at[0], sibling)
    across.start()
    far[OWN, c] = pooled[c]

    halves = []
    for n, (src, dst) in enumerate(((k_hbm, kb), (v_hbm, vb), (q_hbm, qb))):
        cp = remote(src.at[:, :, pl.ds(hi, HALF)], dst.at[mine], sib_ss.at[n], sib_rs.at[n], sibling)
        cp.start()
        halves.append(cp)

    def wait_half(n):
        local[n].wait()
        other = (kb, vb, qb)[n].at[pl.ds(2 * (1 - c), 2)]
        remote(other, other, sib_ss.at[n], sib_rs.at[n], sibling).wait_recv()

    clip_copy.wait()
    row = y * NC + c
    lane = iota((1, 128), 1)
    level_clips[row] = sum(
        jnp.where(lane == 2 * row + n, clip_ref[n].astype(jnp.float32), 0.0) for n in range(2)
    )
    level_sends = []
    for n in range(1, NY * NC):
        to = lax.rem(row + n, NY * NC)
        ref = level_clips.at[row]
        cp = remote(ref, ref, cy_ss.at[n], cy_rs.at[n], z * (NY * NC) + to)
        cp.start()
        level_sends.append(cp)

    near_pool = pool_matrix(NEAR_ROWS * FPC, FPC, 2)
    for n, full in enumerate((kb, vb)):
        wait_half(n)
        near[n, 2 * NEAR_ROWS :] = nn(near_pool, full[...].reshape(ROWS, HALF)).astype(jnp.bfloat16)

    near_out = remote(
        near.at[:, pl.ds(4 * NEAR_ROWS, 2 * NEAR_ROWS)], near.at[:, pl.ds(0, 2 * NEAR_ROWS)],
        near_ss.at[0], near_rs.at[0], jnp.minimum((chip + 1) * NC + c, NZ * NY * NC - 1),
    )

    @pl.when(chip < NZ * NY - 1)
    def _():
        near_out.start()

    for n in range(1, NY * NC):
        ref = level_clips.at[lax.rem(row + NY * NC - n, NY * NC)]
        remote(ref, ref, cy_ss.at[n], cy_rs.at[n], d).wait_recv()
    clips[LEVELS + 1] = jnp.sum(level_clips[...], axis=0)
    for k in range(1, LEVELS + 2):
        @pl.when(z + k < NZ)
        def _():
            remote(
                clips.at[LEVELS + 1], clips.at[LEVELS + 1 - k], cz_ss.at[k], cz_rs.at[k], dev(z + k, y, c)
            ).start()

    def spread(k, delta):
        ref = far.at[slot(k, y)]
        return remote(ref, ref, y_ss.at[k, delta], y_rs.at[k, delta], dev(z, lax.rem(y + delta, NY), c))

    def arrived(k, part):
        ref = far.at[slot(k, y), part]
        remote(ref, ref, z_ss.at[k, 0], z_rs.at[k, part], d).wait_recv()

    def arrived_whole(k):
        ref = far.at[slot(k, y)]
        remote(ref, ref, z_ss.at[k, 0], z_rs.at[k, 0], d).wait_recv()

    def forward():
        return remote(far.at[slot(2, y)], far.at[slot(3, y)], z_ss.at[3, 0], z_rs.at[3, 0], dev(z + 1, y, c))

    def backward():
        return remote(far.at[slot(5, y)], far.at[slot(4, y)], z_ss.at[4, 0], z_rs.at[4, 0], dev(z - 1, y, c))

    def spread_to(k):
        return (1, 3) if k in CHAINED else (1, 3, 2)

    def pass_on(k):
        @pl.when(z >= k)
        def _():
            if k in DIRECT:
                for part in range(NC):
                    arrived(k, part)
            elif k == LEVELS:
                @pl.when(z == NZ - 1)
                def _():
                    for part in range(NC):
                        arrived(k, part)

                @pl.when(z < NZ - 1)
                def _():
                    arrived_whole(k)
            else:
                arrived_whole(k)
            if k == 2:
                @pl.when(z < NZ - 1)
                def _():
                    forward().start()
            if k == LEVELS + 1:
                backward().start()
            for delta in spread_to(k):
                if k <= LEVELS:
                    spread(k, delta).start()
                else:
                    @pl.when(y + delta >= NY)
                    def _():
                        spread(k, delta).start()

    opposite = lax.rem(y + 2, NY)

    def chain(k):
        return remote(
            far.at[slot(k - 1, opposite)], far.at[slot(k, opposite)], x_ss.at[k], y_rs.at[k, 2], dev(z + 1, y, c)
        )

    def came(k, delta):
        ref = far.at[slot(k, lax.rem(y + NY - delta, NY))]
        remote(ref, ref, y_ss.at[k, delta], y_rs.at[k, delta], d).wait_recv()

    def chain_on(k):
        if k not in CHAINED:
            return

        @pl.when(z >= k - 1)
        def _():
            came(k - 1, 2)

            @pl.when(z < NZ - 1)
            def _():
                chain(k).start()

    pass_on(1)

    wait_half(2)
    even = iota((TOK, 128), 1) < HEAD_DIM
    for p in range(PAIRS):
        for i in range(FPC):
            part = qb[i, :, p * 128 : (p + 1) * 128] * jnp.bfloat16(HEAD_DIM ** -0.5)
            apart = jnp.concatenate(
                [jnp.where(even, part, jnp.zeros_like(part)), jnp.where(even, jnp.zeros_like(part), part)], axis=0
            )
            qm[p, :, i * 128 : (i + 1) * 128] = apart.T

    first_head = lax.rem(iota((1, LANES), 1), 128) < TOK

    def pick_head(both):
        return jnp.where(first_head, both[:HEAD_DIM], both[HEAD_DIM:])

    def cols(p):
        return pl.ds(pl.multiple_of(p * 128, 128), 128)

    def own_frame(p, carry):
        qp = qm[p]
        scores = jnp.concatenate(
            [nn(kb[i, :, cols(p)], qp[:, i * 128 : (i + 1) * 128]) for i in range(FPC)], axis=1
        )
        top = jnp.max(scores, axis=0, keepdims=True)
        weights = jnp.exp(scores - top)
        tops[p] = top
        sums[p] = jnp.sum(weights, axis=0, keepdims=True)
        weights = weights.astype(jnp.bfloat16)
        both = jnp.concatenate(
            [tn(vb[i, :, cols(p)], weights[:, i * 128 : (i + 1) * 128]) for i in range(FPC)], axis=1
        )
        acc[p] = pick_head(both)
        return carry

    pass_on(2)
    pass_on(5)
    lax.fori_loop(0, 3, own_frame, 0)
    chain_on(2)
    pass_on(3)
    pass_on(4)
    lax.fori_loop(3, PAIRS, own_frame, 0)

    for k in range(1, LEVELS + 2):
        @pl.when(z >= k)
        def _():
            ref = clips.at[LEVELS + 1 - k]
            remote(ref, ref, cz_ss.at[k], cz_rs.at[k], d).wait_recv()
    table = clips[...].reshape(8, 128)
    own_first = BASE + 4 * y
    query_clip = [
        jnp.sum(jnp.where(lane == 4 * y + i, table[LEVELS + 1 : LEVELS + 2], 0.0), axis=1, keepdims=True)
        for i in range(FPC)
    ]
    table = table.astype(jnp.bfloat16)
    ones = jnp.ones((128, 128), jnp.bfloat16)

    def key_clips(numbers, rows):
        pick = (numbers // (NY * FPC))[:, :8] == iota((rows, 8), 1)
        level = jnp.dot(pick.astype(jnp.float32).astype(jnp.bfloat16), table, preferred_element_type=jnp.float32)
        one = jnp.where(lax.rem(numbers, NY * FPC) == iota((rows, 128), 1), level, 0.0)
        return jnp.dot(one.astype(jnp.bfloat16), ones, preferred_element_type=jnp.float32)

    def far_numbers(shape):
        n = iota(shape, 0)
        at, frame = n // BLK, lax.rem(n, BLK) // FAR
        step = at + NY - 1
        col = lax.rem(step, NY)
        level = functools.reduce(
            lambda found, k: jnp.where(step // NY == ORDER.index(k) + 1, k, found), ORDER, 0
        )
        regular = (LEVELS + 1 - level) * (NY * FPC) + col * FPC + frame
        shared = jnp.where(col < y, BASE, 0) + col * FPC + frame
        held = jnp.where((at >= MIXED) & (at < MIXED + NY), shared, regular)
        return jnp.where(at == OWN, own_first + frame, held)

    def near_numbers(shape):
        return own_first - 2 + iota(shape, 0) // NEAR_ROWS

    floor = (LEVELS + 1 - z) * (NY * FPC)
    for numbers, rows, bias in ((near_numbers, NKN, bias_near), (far_numbers, NKF, bias_far)):
        number = numbers((rows, 128))
        clip_of = key_clips(number, rows)
        for i in range(FPC):
            distance = own_first + i - number
            seen = (distance >= 1) & (distance <= 2) if rows == NKN else distance > 2
            ok = seen & (number >= floor) & (clip_of == query_clip[i])
            bias[:, i * 128 : (i + 1) * 128] = jnp.where(ok, 0.0, NEG)

    @pl.when(chip > 0)
    def _():
        ref = near.at[:, pl.ds(0, 2 * NEAR_ROWS)]
        remote(ref, ref, near_ss.at[0], near_rs.at[0], d).wait_recv()

    chain_on(3)

    def level_here(k):
        @pl.when(z >= k)
        def _():
            for delta in range(1, NY):
                if not (delta == 2 and k + 1 in CHAINED):
                    came(k, delta)

    level_here(1)
    level_here(2)
    for delta in range(1, NY):
        @pl.when(y >= delta)
        def _():
            for part in range(NC):
                ref = far.at[MIXED + lax.rem(y + NY - delta, NY), part]
                remote(ref, ref, m_ss.at[delta, 0], m_rs.at[delta, part], d).wait_recv()

        @pl.when((y < delta) & (z >= LEVELS + 1))
        def _():
            came(LEVELS + 1, delta)
    ref = far.at[OWN, 1 - c]
    remote(ref, ref, own_ss.at[0], own_rs.at[0], d).wait_recv()

    theirs = pl.ds(2 * (1 - c), 2)

    def out_local(p):
        return pltpu.make_async_copy(
            ob.at[p, mine], out_hbm.at[:, :, pl.ds(pl.multiple_of(lo + p * 128, 128), 128)], o_ls.at[p]
        )

    def out_remote(p):
        return remote(
            ob.at[p, theirs], out_hbm.at[:, :, pl.ds(pl.multiple_of(lo + p * 128, 128), 128)],
            o_ss.at[p], o_rs.at[p], sibling,
        )

    def far_rows(p, first, last):
        rows = (last - first) * BLK
        both = far[first:last, :, :, cols(p)].astype(jnp.float32).reshape(rows // 8, 2, 8, 128)
        return [both[:, n].reshape(rows, 128).astype(jnp.bfloat16) for n in range(2)]

    def join(p, scores, values):
        old = tops[p]
        top = functools.reduce(jnp.maximum, [jnp.max(s, axis=0, keepdims=True) for s in scores], old)
        factor = jnp.exp(old - top)
        total = sums[p] * factor
        both = 0.0
        for s, v in zip(scores, values):
            weights = jnp.exp(s - top)
            total = total + jnp.sum(weights, axis=0, keepdims=True)
            both = both + tn(v, weights.astype(jnp.bfloat16))
        return top, total, acc[p] * factor + pick_head(both)

    def early(p, carry):
        keys, values = far_rows(p, 0, EARLY)
        scores = [nn(near[0, :NKN, cols(p)], qm[p]) + bias_near[...], nn(keys, qm[p]) + bias_far[: EARLY * BLK]]
        tops[p], sums[p], acc[p] = join(p, scores, [near[1, :NKN, cols(p)], values])
        return carry

    def late(p):
        keys, values = far_rows(p, EARLY, SLOTS)
        _, total, summed = join(p, [nn(keys, qm[p]) + bias_far[EARLY * BLK :]], [values])
        result = summed / total
        apart = jnp.concatenate(
            [jnp.where(first_head, result, 0.0), jnp.where(first_head, 0.0, result)], axis=0
        ).astype(jnp.bfloat16)
        for i in range(FPC):
            turned = apart[:, i * 128 : (i + 1) * 128].T
            ob[p, i] = turned[:TOK] + turned[TOK:]

    lax.fori_loop(0, PAIRS, early, 0)
    level_here(3)
    level_here(4)
    for group in range(0, PAIRS, 3):
        for p in range(group, group + 3):
            late(p)
        for p in range(group, group + 3):
            out_remote(p).start()
            out_local(p).start()

    for p in range(PAIRS):
        out_local(p).wait()
        out_remote(p).wait_send()
        ref = out_hbm.at[:, :, pl.ds(pl.multiple_of(hi + p * 128, 128), 128)]
        remote(ref, ref, o_ss.at[p], o_rs.at[p], sibling).wait_recv()
    for n in range(3):
        halves[n].wait_send()
    for cp in level_sends:
        cp.wait_send()
    across.wait_send()
    each_rise(lambda cp: cp.wait_send())
    each_mixed(lambda cp: cp.wait_send())

    @pl.when(z >= LEVELS + 1)
    def _():
        backward().wait_send()

    @pl.when((z >= 2) & (z < NZ - 1))
    def _():
        forward().wait_send()

    for k in CHAINED:
        @pl.when((z >= k - 1) & (z < NZ - 1))
        def _():
            chain(k).wait_send()

    for k in range(1, LEVELS + 2):
        @pl.when(z + k < NZ)
        def _():
            remote(clips.at[LEVELS + 1], clips.at[LEVELS + 1 - k], cz_ss.at[k], cz_rs.at[k], d).wait_send()

    @pl.when(chip < NZ * NY - 1)
    def _():
        near_out.wait_send()

    for k in ORDER:
        for delta in spread_to(k):
            @pl.when((z >= k) if k <= LEVELS else ((z >= k) & (y + delta >= NY)))
            def _():
                spread(k, delta).wait_send()


def on_device(queries, key_states, value_states, clip_ids):
    bf, f32 = jnp.bfloat16, jnp.float32
    dma = pltpu.SemaphoreType.DMA
    anywhere = pl.BlockSpec(memory_space=pltpu.HBM)
    return pl.pallas_call(
        kernel,
        out_shape=jax.ShapeDtypeStruct(queries.shape, bf),
        in_specs=[anywhere] * 4,
        out_specs=anywhere,
        scratch_shapes=[
            pltpu.SMEM((2,), jnp.int32),
            pltpu.VMEM((2, TOK, 2 * HALF), bf),
            pltpu.VMEM((2, TOK, 2 * HALF), bf),
            pltpu.VMEM((FPC, TOK, HALF), bf),
            pltpu.VMEM((FPC, TOK, HALF), bf),
            pltpu.VMEM((FPC, TOK, HALF), bf),
            pltpu.VMEM((2, BLK, HALF), bf),
            pltpu.VMEM((SLOTS, NC, BLK, HALF), bf),
            pltpu.VMEM((2, 6 * NEAR_ROWS, HALF), bf),
            pltpu.VMEM((PAIRS, 128, LANES), bf),
            pltpu.VMEM((NY * NC, 1, 128), f32),
            pltpu.VMEM((8, 1, 128), f32),
            pltpu.VMEM((NKF, LANES), f32),
            pltpu.VMEM((NKN, LANES), f32),
            pltpu.VMEM((PAIRS, HEAD_DIM, LANES), f32),
            pltpu.VMEM((PAIRS, 1, LANES), f32),
            pltpu.VMEM((PAIRS, 1, LANES), f32),
            pltpu.VMEM((PAIRS, FPC, TOK, 128), bf),
            dma((6,)),
            dma((3,)), dma((3,)),
            dma((1,)), dma((1,)),
            dma((LEVELS + 2, NC)), dma((LEVELS + 2, NC)),
            dma((NY, NC)), dma((NY, NC)),
            dma((LEVELS + 2, NY)), dma((LEVELS + 2, NY)), dma((LEVELS + 2,)),
            dma((1,)), dma((1,)),
            dma((NY * NC,)), dma((NY * NC,)),
            dma((LEVELS + 2,)), dma((LEVELS + 2,)),
            dma((PAIRS,)), dma((PAIRS,)), dma((PAIRS,)),
        ],
        compiler_params=pltpu.CompilerParams(
            collective_id=0, has_side_effects=True, vmem_limit_bytes=64 << 20
        ),
        cost_estimate=pl.CostEstimate(flops=1 << 30, bytes_accessed=4 << 20, transcendentals=1 << 21),
    )(queries, key_states, value_states, clip_ids)


def solution(mesh):
    frames = P(("dp", "tm"), None, None)
    return jax.shard_map(
        on_device,
        mesh=mesh,
        in_specs=(frames, frames, frames, P(("dp", "tm"))),
        out_specs=frames,
        check_vma=False,
    )
```

time: 32.3 us -> 29.2 us (0.904)
  the two profiles are of different devices: /device:TPU:163 before, /device:TPU:71 now
where the time goes in v3:
time: 29.2 us; the launch traced here: 29 us
  Pallas kernels  27.2 us (93%)
  local copies, waits for them, and re-layouts  1.77 us (6%)
    pallas_call x1, Pallas kernels, on_device(): pl.pallas_call(kernel, out_shape=jax.ShapeDtypeStruct(queries.shape, bf),...  27.2 us
    unnamed x1, local copies, waits for them, and re-layouts  1.77 us

profile of v3, /device:TPU:71, one launch (start us, length us, event | category | flops | bytes accessed | tf_op | source)
XLA Modules:
  0.0 29.0 jit_solution(7009288011015073726)
XLA Ops:
  0.0 27.2 %shard_map.46 = bf16[2,64,1536]{2,1,0:T(8,128)(2,1)} custom-call(bf16[2,64,1536]{2,1,0:T(8,128)(2,1)} %q_hbm.1, bf16[2,64,1536]{2,1,0:T(8,128)(2,1)} %k_hbm.1, bf16[2,64,1536]{2,1,0:T(8,128)(2,1)} %v_hbm.1, s32[2]{0:T(128)} %clip_hbm.1), custom_call_target="tpu_custom_call" | custom-call | flops 1073741824 | bytes 4194304 | tf_op jit(solution)/shard_map/pallas_call | solution.py:529
  27.3 1.8 %copy.6 = bf16[2,64,1536]{2,1,0:T(8,128)(2,1)} copy(bf16[2,64,1536]{2,1,0:T(8,128)(2,1)} %shard_map.46) | data formatting | bytes 786432

commit v4 on v3

--- a/solution.py
+++ b/solution.py
@@ -23,10 +23,10 @@
 ORDER = (1, 2, 5, 3, 4)
 FIRST = {k: 1 + n * NY for n, k in enumerate(ORDER)}
 DIRECT = (1, 2, 5)
-CHAINED = (2, 3)
+CHAINED = (2,)
 MIXED = FIRST[LEVELS + 1]
 SLOTS = 1 + 5 * NY
-EARLY = FIRST[3]
+CHUNKS = (FIRST[2], FIRST[3])
 NKF = SLOTS * BLK
 NEAR_ROWS = 16
 NKN = 5 * NEAR_ROWS
@@ -72,6 +72,33 @@
         return zz * (NY * NC) + yy * NC + cc
 
     sibling = dev(z, y, 1 - c)
+
+    barrier = pltpu.get_barrier_semaphore()
+
+    def greet(to):
+        pl.semaphore_signal(barrier, inc=1, device_id={"tm": to}, device_id_type=MESH)
+
+    for k in range(LEVELS + 1, 0, -1):
+        @pl.when(z >= k)
+        def _():
+            greet(dev(z - k, y, c))
+            if k in DIRECT:
+                greet(dev(z - k, y, 1 - c))
+
+    last_rise = NZ - 1 - LEVELS
+
+    @pl.when(z == NZ - 1)
+    def _():
+        greet(dev(last_rise, y, 1 - c))
+
+    @pl.when((y == 0) & (z > 0))
+    def _():
+        greet(dev(z - 1, NY - 1, c))
+
+    for yy in range(1, NY):
+        for cc in range(NC):
+            greet(dev(z, lax.rem(y + yy, NY), cc))
+    greet(sibling)
 
     lo = pl.multiple_of(c * HALF, 128)
     hi = pl.multiple_of((1 - c) * HALF, 128)
@@ -89,35 +116,22 @@
         cp.start()
         local.append(cp)
 
-    far[...] = jnp.zeros_like(far)
-    near[:, : 2 * NEAR_ROWS] = jnp.zeros((2, 2 * NEAR_ROWS, HALF), jnp.bfloat16)
-    clips[...] = jnp.zeros_like(clips)
-
-    barrier = pltpu.get_barrier_semaphore()
-
-    def greet(to):
-        pl.semaphore_signal(barrier, inc=1, device_id={"tm": to}, device_id_type=MESH)
-
-    for yy in range(1, NY):
-        for cc in range(NC):
-            greet(dev(z, lax.rem(y + yy, NY), cc))
-    greet(sibling)
+    for k in ORDER:
+        for col in range(NY):
+            @pl.when((z < k) & (col >= y) if k == LEVELS + 1 else z < k)
+            def _():
+                far[FIRST[k] + col] = jnp.zeros(far.shape[1:], far.dtype)
+
+    @pl.when(chip == 0)
+    def _():
+        near[:, : 2 * NEAR_ROWS] = jnp.zeros((2, 2 * NEAR_ROWS, HALF), jnp.bfloat16)
+
     for k in range(1, LEVELS + 2):
-        @pl.when(z >= k)
-        def _():
-            greet(dev(z - k, y, c))
-            if k in DIRECT:
-                greet(dev(z - k, y, 1 - c))
-
-    last_rise = NZ - 1 - LEVELS
-
-    @pl.when(z == NZ - 1)
-    def _():
-        greet(dev(last_rise, y, 1 - c))
-
-    @pl.when((y == 0) & (z > 0))
-    def _():
-        greet(dev(z - 1, NY - 1, c))
+        @pl.when(z < k)
+        def _():
+            clips[LEVELS + 1 - k] = jnp.zeros((1, 128), jnp.float32)
+    for n in range(LEVELS + 2, 8):
+        clips[n] = jnp.zeros((1, 128), jnp.float32)
 
     def pool_matrix(rows, frames, side):
         r, t = iota((rows, frames * TOK), 0), iota((rows, frames * TOK), 1)
@@ -248,7 +262,7 @@
         return remote(far.at[slot(5, y)], far.at[slot(4, y)], z_ss.at[4, 0], z_rs.at[4, 0], dev(z - 1, y, c))
 
     def spread_to(k):
-        return (1, 3) if k in CHAINED else (1, 3, 2)
+        return (1, 3) if k in CHAINED else (2, 1, 3)
 
     def pass_on(k):
         @pl.when(z >= k)
@@ -307,46 +321,56 @@
     pass_on(1)
 
     wait_half(2)
-    even = iota((TOK, 128), 1) < HEAD_DIM
-    for p in range(PAIRS):
-        for i in range(FPC):
-            part = qb[i, :, p * 128 : (p + 1) * 128] * jnp.bfloat16(HEAD_DIM ** -0.5)
-            apart = jnp.concatenate(
-                [jnp.where(even, part, jnp.zeros_like(part)), jnp.where(even, jnp.zeros_like(part), part)], axis=0
-            )
-            qm[p, :, i * 128 : (i + 1) * 128] = apart.T
-
-    first_head = lax.rem(iota((1, LANES), 1), 128) < TOK
-
-    def pick_head(both):
-        return jnp.where(first_head, both[:HEAD_DIM], both[HEAD_DIM:])
 
     def cols(p):
         return pl.ds(pl.multiple_of(p * 128, 128), 128)
 
+    def lanes(head, group):
+        return slice(head * ROWS + group * 128, head * ROWS + (group + 1) * 128)
+
+    first_rows = iota((128, 128), 0) < HEAD_DIM
+    nothing = jnp.zeros((128, 128), jnp.bfloat16)
+    for p in range(PAIRS):
+        for group in range(2):
+            part = qb[2 * group : 2 * group + 2, :, p * 128 : (p + 1) * 128].reshape(128, 128)
+            turned = (part * jnp.bfloat16(HEAD_DIM ** -0.5)).T
+            qm[p, :, lanes(0, group)] = jnp.where(first_rows, turned, nothing)
+            qm[p, :, lanes(1, group)] = jnp.where(first_rows, nothing, turned)
+
+    first_frame = iota((1, 128), 1) < TOK
+
     def own_frame(p, carry):
-        qp = qm[p]
-        scores = jnp.concatenate(
-            [nn(kb[i, :, cols(p)], qp[:, i * 128 : (i + 1) * 128]) for i in range(FPC)], axis=1
-        )
+        def two_frames(ref, group):
+            return ref[2 * group : 2 * group + 2, :, cols(p)].reshape(128, 128)
+
+        keys = [two_frames(kb, group) for group in range(2)]
+        values = [two_frames(vb, group) for group in range(2)]
+        scores = []
+        for head in range(2):
+            for group in range(2):
+                both = nn(keys[group], qm[p, :, lanes(head, group)])
+                scores.append(jnp.where(first_frame, both[:TOK], both[TOK:]))
+        scores = jnp.concatenate(scores, axis=1)
         top = jnp.max(scores, axis=0, keepdims=True)
         weights = jnp.exp(scores - top)
         tops[p] = top
         sums[p] = jnp.sum(weights, axis=0, keepdims=True)
-        weights = weights.astype(jnp.bfloat16)
-        both = jnp.concatenate(
-            [tn(vb[i, :, cols(p)], weights[:, i * 128 : (i + 1) * 128]) for i in range(FPC)], axis=1
-        )
-        acc[p] = pick_head(both)
+        for head in range(2):
+            for group in range(2):
+                part = weights[:, lanes(head, group)]
+                apart = jnp.concatenate(
+                    [jnp.where(first_frame, part, 0.0), jnp.where(first_frame, 0.0, part)], axis=0
+                ).astype(jnp.bfloat16)
+                acc[p, :, lanes(head, group)] = tn(values[group], apart)[head * HEAD_DIM : (head + 1) * HEAD_DIM]
         return carry
 
     pass_on(2)
     pass_on(5)
-    lax.fori_loop(0, 3, own_frame, 0)
+    lax.fori_loop(0, 3, own_frame, 0, unroll=3)
     chain_on(2)
     pass_on(3)
     pass_on(4)
-    lax.fori_loop(3, PAIRS, own_frame, 0)
+    lax.fori_loop(3, PAIRS, own_frame, 0, unroll=3)
 
     for k in range(1, LEVELS + 2):
         @pl.when(z >= k)
@@ -388,11 +412,12 @@
     for numbers, rows, bias in ((near_numbers, NKN, bias_near), (far_numbers, NKF, bias_far)):
         number = numbers((rows, 128))
         clip_of = key_clips(number, rows)
-        for i in range(FPC):
-            distance = own_first + i - number
+        for group in range(2):
+            distance = own_first + 2 * group + lane // TOK - number
             seen = (distance >= 1) & (distance <= 2) if rows == NKN else distance > 2
-            ok = seen & (number >= floor) & (clip_of == query_clip[i])
-            bias[:, i * 128 : (i + 1) * 128] = jnp.where(ok, 0.0, NEG)
+            clip_here = jnp.where(first_frame, query_clip[2 * group], query_clip[2 * group + 1])
+            ok = seen & (number >= floor) & (clip_of == clip_here)
+            bias[:, group * 128 : (group + 1) * 128] = jnp.where(ok, 0.0, NEG)
 
     @pl.when(chip > 0)
     def _():
@@ -408,18 +433,18 @@
                 if not (delta == 2 and k + 1 in CHAINED):
                     came(k, delta)
 
-    level_here(1)
-    level_here(2)
-    for delta in range(1, NY):
-        @pl.when(y >= delta)
-        def _():
-            for part in range(NC):
-                ref = far.at[MIXED + lax.rem(y + NY - delta, NY), part]
-                remote(ref, ref, m_ss.at[delta, 0], m_rs.at[delta, part], d).wait_recv()
-
-        @pl.when((y < delta) & (z >= LEVELS + 1))
-        def _():
-            came(LEVELS + 1, delta)
+    def shared_here():
+        for delta in range(1, NY):
+            @pl.when(y >= delta)
+            def _():
+                for part in range(NC):
+                    ref = far.at[MIXED + lax.rem(y + NY - delta, NY), part]
+                    remote(ref, ref, m_ss.at[delta, 0], m_rs.at[delta, part], d).wait_recv()
+
+            @pl.when((y < delta) & (z >= LEVELS + 1))
+            def _():
+                came(LEVELS + 1, delta)
+
     ref = far.at[OWN, 1 - c]
     remote(ref, ref, own_ss.at[0], own_rs.at[0], d).wait_recv()
 
@@ -441,44 +466,68 @@
         both = far[first:last, :, :, cols(p)].astype(jnp.float32).reshape(rows // 8, 2, 8, 128)
         return [both[:, n].reshape(rows, 128).astype(jnp.bfloat16) for n in range(2)]
 
-    def join(p, scores, values):
+    def join(p, keys, values, bias):
+        scores = nn(keys, qm[p]) + jnp.concatenate([bias, bias], axis=1)
         old = tops[p]
-        top = functools.reduce(jnp.maximum, [jnp.max(s, axis=0, keepdims=True) for s in scores], old)
+        top = jnp.maximum(old, jnp.max(scores, axis=0, keepdims=True))
         factor = jnp.exp(old - top)
-        total = sums[p] * factor
-        both = 0.0
-        for s, v in zip(scores, values):
-            weights = jnp.exp(s - top)
-            total = total + jnp.sum(weights, axis=0, keepdims=True)
-            both = both + tn(v, weights.astype(jnp.bfloat16))
-        return top, total, acc[p] * factor + pick_head(both)
-
-    def early(p, carry):
-        keys, values = far_rows(p, 0, EARLY)
-        scores = [nn(near[0, :NKN, cols(p)], qm[p]) + bias_near[...], nn(keys, qm[p]) + bias_far[: EARLY * BLK]]
-        tops[p], sums[p], acc[p] = join(p, scores, [near[1, :NKN, cols(p)], values])
-        return carry
-
-    def late(p):
-        keys, values = far_rows(p, EARLY, SLOTS)
-        _, total, summed = join(p, [nn(keys, qm[p]) + bias_far[EARLY * BLK :]], [values])
-        result = summed / total
-        apart = jnp.concatenate(
-            [jnp.where(first_head, result, 0.0), jnp.where(first_head, 0.0, result)], axis=0
-        ).astype(jnp.bfloat16)
-        for i in range(FPC):
-            turned = apart[:, i * 128 : (i + 1) * 128].T
-            ob[p, i] = turned[:TOK] + turned[TOK:]
-
-    lax.fori_loop(0, PAIRS, early, 0)
+        weights = jnp.exp(scores - top)
+        total = sums[p] * factor + jnp.sum(weights, axis=0, keepdims=True)
+        weights = weights.astype(jnp.bfloat16)
+        turned = values.T
+        summed = [
+            nn(turned[n * HEAD_DIM : (n + 1) * HEAD_DIM], weights[:, n * ROWS : (n + 1) * ROWS]) for n in range(2)
+        ]
+        return top, total, acc[p] * factor + jnp.concatenate(summed, axis=1)
+
+    def keep(part):
+        joined = [join(p, *part(p)) for p in range(PAIRS)]
+        for p, (top, total, summed) in enumerate(joined):
+            tops[p], sums[p], acc[p] = top, total, summed
+
+    def nearest(p):
+        keys, values = far_rows(p, 0, CHUNKS[0])
+        keys = jnp.concatenate([near[0, :NKN, cols(p)], keys], axis=0)
+        values = jnp.concatenate([near[1, :NKN, cols(p)], values], axis=0)
+        return keys, values, jnp.concatenate([bias_near[...], bias_far[: CHUNKS[0] * BLK]], axis=0)
+
+    def middle(p):
+        return *far_rows(p, *CHUNKS), bias_far[CHUNKS[0] * BLK : CHUNKS[1] * BLK]
+
+    def put(p, total, summed):
+        result = (summed / total).astype(jnp.bfloat16)
+        for group in range(2):
+            turned = jnp.concatenate([result[:, lanes(head, group)] for head in range(2)], axis=0).T
+            ob[p, 2 * group] = turned[:TOK]
+            ob[p, 2 * group + 1] = turned[TOK:]
+
+    level_here(1)
+    keep(nearest)
+    level_here(2)
+    shared_here()
+    keep(middle)
     level_here(3)
     level_here(4)
-    for group in range(0, PAIRS, 3):
-        for p in range(group, group + 3):
-            late(p)
-        for p in range(group, group + 3):
+    def send_out(group):
+        for p in group:
             out_remote(p).start()
             out_local(p).start()
+
+    groups = (range(0, 3), range(3, PAIRS))
+
+    @pl.when(z >= 3)
+    def _():
+        for group in groups:
+            for p in group:
+                put(p, *join(p, *far_rows(p, CHUNKS[1], SLOTS), bias_far[CHUNKS[1] * BLK :])[1:])
+            send_out(group)
+
+    @pl.when(z < 3)
+    def _():
+        for group in groups:
+            for p in group:
+                put(p, sums[p], acc[p])
+            send_out(group)
 
     for p in range(PAIRS):
         out_local(p).wait()
@@ -544,8 +593,8 @@
             pltpu.VMEM((PAIRS, 128, LANES), bf),
             pltpu.VMEM((NY * NC, 1, 128), f32),
             pltpu.VMEM((8, 1, 128), f32),
-            pltpu.VMEM((NKF, LANES), f32),
-            pltpu.VMEM((NKN, LANES), f32),
+            pltpu.VMEM((NKF, ROWS), f32),
+            pltpu.VMEM((NKN, ROWS), f32),
             pltpu.VMEM((PAIRS, HEAD_DIM, LANES), f32),
             pltpu.VMEM((PAIRS, 1, LANES), f32),
             pltpu.VMEM((PAIRS, 1, LANES), f32),

time: 29.2 us -> 27.9 us (0.955)
  the two profiles are of different devices: /device:TPU:71 before, /device:TPU:163 now
where the time goes in v4:
time: 27.9 us; the launch traced here: 27.7 us
  Pallas kernels  25.9 us (93%)
  local copies, waits for them, and re-layouts  1.77 us (6%)
    pallas_call x1, Pallas kernels, on_device(): pl.pallas_call(kernel, out_shape=jax.ShapeDtypeStruct(queries.shape, bf),...  25.9 us
    unnamed x1, local copies, waits for them, and re-layouts  1.77 us

profile of v4, /device:TPU:163, one launch (start us, length us, event | category | flops | bytes accessed | tf_op | source)
XLA Modules:
  0.0 27.7 jit_solution(12912851376315015859)
XLA Ops:
  0.0 25.9 %shard_map.46 = bf16[2,64,1536]{2,1,0:T(8,128)(2,1)} custom-call(bf16[2,64,1536]{2,1,0:T(8,128)(2,1)} %q_hbm.1, bf16[2,64,1536]{2,1,0:T(8,128)(2,1)} %k_hbm.1, bf16[2,64,1536]{2,1,0:T(8,128)(2,1)} %v_hbm.1, s32[2]{0:T(128)} %clip_hbm.1), custom_call_target="tpu_custom_call" | custom-call | flops 1073741824 | bytes 4194304 | tf_op jit(solution)/shard_map/pallas_call | solution.py:578
  26.0 1.8 %copy.6 = bf16[2,64,1536]{2,1,0:T(8,128)(2,1)} copy(bf16[2,64,1536]{2,1,0:T(8,128)(2,1)} %shard_map.46) | data formatting | bytes 786432

commit v5 on v4

--- a/solution.py
+++ b/solution.py
@@ -23,6 +23,7 @@
 ORDER = (1, 2, 5, 3, 4)
 FIRST = {k: 1 + n * NY for n, k in enumerate(ORDER)}
 DIRECT = (1, 2, 5)
+HALVED = (3, 4)
 CHAINED = (2,)
 MIXED = FIRST[LEVELS + 1]
 SLOTS = 1 + 5 * NY
@@ -243,9 +244,14 @@
                 clips.at[LEVELS + 1], clips.at[LEVELS + 1 - k], cz_ss.at[k], cz_rs.at[k], dev(z + k, y, c)
             ).start()
 
-    def spread(k, delta):
-        ref = far.at[slot(k, y)]
-        return remote(ref, ref, y_ss.at[k, delta], y_rs.at[k, delta], dev(z, lax.rem(y + delta, NY), c))
+    def spread(k, delta, half=None):
+        ref, at = whole_or_half(slot(k, y), half), delta + NY * (half or 0)
+        return remote(ref, ref, y_ss.at[k, at], y_rs.at[k, at], dev(z, lax.rem(y + delta, NY), c))
+
+    def whole_or_half(at, half):
+        if half is None:
+            return far.at[at]
+        return far.at[at, :, :, half * (HALF // 2) : (half + 1) * (HALF // 2)]
 
     def arrived(k, part):
         ref = far.at[slot(k, y), part]
@@ -289,7 +295,7 @@
                 backward().start()
             for delta in spread_to(k):
                 if k <= LEVELS:
-                    spread(k, delta).start()
+                    spread(k, delta, 0 if k in HALVED else None).start()
                 else:
                     @pl.when(y + delta >= NY)
                     def _():
@@ -302,9 +308,9 @@
             far.at[slot(k - 1, opposite)], far.at[slot(k, opposite)], x_ss.at[k], y_rs.at[k, 2], dev(z + 1, y, c)
         )
 
-    def came(k, delta):
-        ref = far.at[slot(k, lax.rem(y + NY - delta, NY))]
-        remote(ref, ref, y_ss.at[k, delta], y_rs.at[k, delta], d).wait_recv()
+    def came(k, delta, half=None):
+        ref, at = whole_or_half(slot(k, lax.rem(y + NY - delta, NY)), half), delta + NY * (half or 0)
+        remote(ref, ref, y_ss.at[k, at], y_rs.at[k, at], d).wait_recv()
 
     def chain_on(k):
         if k not in CHAINED:
@@ -370,6 +376,11 @@
     chain_on(2)
     pass_on(3)
     pass_on(4)
+    for k in HALVED:
+        @pl.when(z >= k)
+        def _():
+            for delta in spread_to(k):
+                spread(k, delta, 1).start()
     lax.fori_loop(3, PAIRS, own_frame, 0, unroll=3)
 
     for k in range(1, LEVELS + 2):
@@ -426,12 +437,12 @@
 
     chain_on(3)
 
-    def level_here(k):
+    def level_here(k, half=None):
         @pl.when(z >= k)
         def _():
             for delta in range(1, NY):
                 if not (delta == 2 and k + 1 in CHAINED):
-                    came(k, delta)
+                    came(k, delta, half)
 
     def shared_here():
         for delta in range(1, NY):
@@ -506,8 +517,6 @@
     level_here(2)
     shared_here()
     keep(middle)
-    level_here(3)
-    level_here(4)
     def send_out(group):
         for p in group:
             out_remote(p).start()
@@ -517,7 +526,9 @@
 
     @pl.when(z >= 3)
     def _():
-        for group in groups:
+        for half, group in enumerate(groups):
+            for k in HALVED:
+                level_here(k, half)
             for p in group:
                 put(p, *join(p, *far_rows(p, CHUNKS[1], SLOTS), bias_far[CHUNKS[1] * BLK :])[1:])
             send_out(group)
@@ -568,7 +579,8 @@
         for delta in spread_to(k):
             @pl.when((z >= k) if k <= LEVELS else ((z >= k) & (y + delta >= NY)))
             def _():
-                spread(k, delta).wait_send()
+                for half in (0, 1) if k in HALVED else (None,):
+                    spread(k, delta, half).wait_send()
 
 
 def on_device(queries, key_states, value_states, clip_ids):
@@ -604,7 +616,7 @@
             dma((1,)), dma((1,)),
             dma((LEVELS + 2, NC)), dma((LEVELS + 2, NC)),
             dma((NY, NC)), dma((NY, NC)),
-            dma((LEVELS + 2, NY)), dma((LEVELS + 2, NY)), dma((LEVELS + 2,)),
+            dma((LEVELS + 2, 2 * NY)), dma((LEVELS + 2, 2 * NY)), dma((LEVELS + 2,)),
             dma((1,)), dma((1,)),
             dma((NY * NC,)), dma((NY * NC,)),
             dma((LEVELS + 2,)), dma((LEVELS + 2,)),

time: 27.9 us -> 27.4 us (0.982)
  Pallas kernels: 25.9 us -> 25.5 us
    pallas_call x1, Pallas kernels: 25.9 us -> 25.5 us  [on_device(): pl.pallas_call(kernel, out_shape=jax.ShapeDtypeStruct(queries.shape, bf),...]
where the time goes in v5:
time: 27.4 us; the launch traced here: 27.2 us
  Pallas kernels  25.5 us (93%)
  local copies, waits for them, and re-layouts  1.77 us (6%)
    pallas_call x1, Pallas kernels, on_device(): pl.pallas_call(kernel, out_shape=jax.ShapeDtypeStruct(queries.shape, bf),...  25.5 us
    unnamed x1, local copies, waits for them, and re-layouts  1.77 us

profile of v5, /device:TPU:163, one launch (start us, length us, event | category | flops | bytes accessed | tf_op | source)
XLA Modules:
  0.0 27.2 jit_solution(1216799849632273715)
XLA Ops:
  0.0 25.5 %shard_map.46 = bf16[2,64,1536]{2,1,0:T(8,128)(2,1)} custom-call(bf16[2,64,1536]{2,1,0:T(8,128)(2,1)} %q_hbm.1, bf16[2,64,1536]{2,1,0:T(8,128)(2,1)} %k_hbm.1, bf16[2,64,1536]{2,1,0:T(8,128)(2,1)} %v_hbm.1, s32[2]{0:T(128)} %clip_hbm.1), custom_call_target="tpu_custom_call" | custom-call | flops 1073741824 | bytes 4194304 | tf_op jit(solution)/shard_map/pallas_call | solution.py:590
  25.5 1.8 %copy.6 = bf16[2,64,1536]{2,1,0:T(8,128)(2,1)} copy(bf16[2,64,1536]{2,1,0:T(8,128)(2,1)} %shard_map.46) | data formatting | bytes 786432

commit v6 on v5

--- a/solution.py
+++ b/solution.py
@@ -23,6 +23,7 @@
 ORDER = (1, 2, 5, 3, 4)
 FIRST = {k: 1 + n * NY for n, k in enumerate(ORDER)}
 DIRECT = (1, 2, 5)
+LEAP = 3
 HALVED = (3, 4)
 CHAINED = (2,)
 MIXED = FIRST[LEVELS + 1]
@@ -79,18 +80,11 @@
     def greet(to):
         pl.semaphore_signal(barrier, inc=1, device_id={"tm": to}, device_id_type=MESH)
 
-    for k in range(LEVELS + 1, 0, -1):
+    for k in DIRECT[::-1]:
         @pl.when(z >= k)
         def _():
-            greet(dev(z - k, y, c))
-            if k in DIRECT:
-                greet(dev(z - k, y, 1 - c))
-
-    last_rise = NZ - 1 - LEVELS
-
-    @pl.when(z == NZ - 1)
-    def _():
-        greet(dev(last_rise, y, 1 - c))
+            for core in range(NC):
+                greet(dev(z - k, y, core))
 
     @pl.when((y == 0) & (z > 0))
     def _():
@@ -128,7 +122,7 @@
         near[:, : 2 * NEAR_ROWS] = jnp.zeros((2, 2 * NEAR_ROWS, HALF), jnp.bfloat16)
 
     for k in range(1, LEVELS + 2):
-        @pl.when(z < k)
+        @pl.when(z < (3 if k == LEVELS else k))
         def _():
             clips[LEVELS + 1 - k] = jnp.zeros((1, 128), jnp.float32)
     for n in range(LEVELS + 2, 8):
@@ -150,10 +144,9 @@
     for n in range(2):
         pooled[n] = means[:, n * HALF : (n + 1) * HALF]
 
-    up = jnp.minimum(NZ - 1 - z, LEVELS + 1)
-    crossing = sum(jnp.where(z + k < NZ, 1, 0) for k in DIRECT) + jnp.where(z == last_rise, 1, 0)
+    up = sum(jnp.where(z + k < NZ, NC, 0) for k in DIRECT)
     next_near = jnp.where((y == NY - 1) & (z < NZ - 1), 1, 0)
-    pl.semaphore_wait(barrier, (NY - 1) * NC + 1 + up + crossing + next_near)
+    pl.semaphore_wait(barrier, (NY - 1) * NC + 1 + up + next_near)
 
     def slot(k, col):
         return FIRST[k] + col
@@ -170,16 +163,11 @@
         )
 
     def each_rise(act):
-        for k in DIRECT:
+        for k in (1, 5, 2):
             @pl.when(z + k < NZ)
             def _():
                 for core in range(NC):
                     act(rise(k, core))
-
-        @pl.when(z == last_rise)
-        def _():
-            for core in range(NC):
-                act(rise(LEVELS, core))
 
     def each_mixed(act):
         for delta in (1, 3, 2):
@@ -237,12 +225,22 @@
         ref = level_clips.at[lax.rem(row + NY * NC - n, NY * NC)]
         remote(ref, ref, cy_ss.at[n], cy_rs.at[n], d).wait_recv()
     clips[LEVELS + 1] = jnp.sum(level_clips[...], axis=0)
-    for k in range(1, LEVELS + 2):
+    def clips_up(k):
+        return remote(
+            clips.at[LEVELS + 1], clips.at[LEVELS + 1 - k], cz_ss.at[k], cz_rs.at[k], dev(z + k, y, c)
+        )
+
+    def clips_on():
+        return remote(clips.at[3:5], clips.at[1:3], cz_ss.at[3], cz_rs.at[3], dev(z + 2, y, c))
+
+    def clips_came(k):
+        ref = clips.at[1:3] if k == 3 else clips.at[LEVELS + 1 - k]
+        remote(ref, ref, cz_ss.at[k], cz_rs.at[k], d).wait_recv()
+
+    for k in DIRECT:
         @pl.when(z + k < NZ)
         def _():
-            remote(
-                clips.at[LEVELS + 1], clips.at[LEVELS + 1 - k], cz_ss.at[k], cz_rs.at[k], dev(z + k, y, c)
-            ).start()
+            clips_up(k).start()
 
     def spread(k, delta, half=None):
         ref, at = whole_or_half(slot(k, y), half), delta + NY * (half or 0)
@@ -264,6 +262,11 @@
     def forward():
         return remote(far.at[slot(2, y)], far.at[slot(3, y)], z_ss.at[3, 0], z_rs.at[3, 0], dev(z + 1, y, c))
 
+    def leap():
+        return remote(
+            far.at[slot(2, y)], far.at[slot(4, y)], z_ss.at[4, 1], z_rs.at[4, 0], dev(jnp.minimum(z + 2, NZ - 1), y, c)
+        )
+
     def backward():
         return remote(far.at[slot(5, y)], far.at[slot(4, y)], z_ss.at[4, 0], z_rs.at[4, 0], dev(z - 1, y, c))
 
@@ -276,23 +279,20 @@
             if k in DIRECT:
                 for part in range(NC):
                     arrived(k, part)
-            elif k == LEVELS:
-                @pl.when(z == NZ - 1)
-                def _():
-                    for part in range(NC):
-                        arrived(k, part)
-
-                @pl.when(z < NZ - 1)
-                def _():
-                    arrived_whole(k)
             else:
                 arrived_whole(k)
             if k == 2:
                 @pl.when(z < NZ - 1)
                 def _():
                     forward().start()
+
+                @pl.when((z >= LEAP) & (z <= NZ - 3))
+                def _():
+                    leap().start()
             if k == LEVELS + 1:
-                backward().start()
+                @pl.when(z < LEAP + 3)
+                def _():
+                    backward().start()
             for delta in spread_to(k):
                 if k <= LEVELS:
                     spread(k, delta, 0 if k in HALVED else None).start()
@@ -372,6 +372,15 @@
 
     pass_on(2)
     pass_on(5)
+    for k in (1, 2):
+        @pl.when(z >= k)
+        def _():
+            clips_came(k)
+
+    @pl.when((z >= 1) & (z < NZ - 2))
+    def _():
+        clips_on().start()
+
     lax.fori_loop(0, 3, own_frame, 0, unroll=3)
     chain_on(2)
     pass_on(3)
@@ -383,11 +392,10 @@
                 spread(k, delta, 1).start()
     lax.fori_loop(3, PAIRS, own_frame, 0, unroll=3)
 
-    for k in range(1, LEVELS + 2):
+    for k in (3, LEVELS + 1):
         @pl.when(z >= k)
         def _():
-            ref = clips.at[LEVELS + 1 - k]
-            remote(ref, ref, cz_ss.at[k], cz_rs.at[k], d).wait_recv()
+            clips_came(k)
     table = clips[...].reshape(8, 128)
     own_first = BASE + 4 * y
     query_clip = [
@@ -553,7 +561,7 @@
     each_rise(lambda cp: cp.wait_send())
     each_mixed(lambda cp: cp.wait_send())
 
-    @pl.when(z >= LEVELS + 1)
+    @pl.when((z >= LEVELS + 1) & (z < LEAP + 3))
     def _():
         backward().wait_send()
 
@@ -566,10 +574,18 @@
         def _():
             chain(k).wait_send()
 
-    for k in range(1, LEVELS + 2):
+    for k in DIRECT:
         @pl.when(z + k < NZ)
         def _():
-            remote(clips.at[LEVELS + 1], clips.at[LEVELS + 1 - k], cz_ss.at[k], cz_rs.at[k], d).wait_send()
+            clips_up(k).wait_send()
+
+    @pl.when((z >= 1) & (z < NZ - 2))
+    def _():
+        clips_on().wait_send()
+
+    @pl.when((z >= LEAP) & (z <= NZ - 3))
+    def _():
+        leap().wait_send()
 
     @pl.when(chip < NZ * NY - 1)
     def _():

time: 27.4 us -> 27 us (0.985)
  Pallas kernels: 25.5 us -> 25.1 us
    pallas_call x1, Pallas kernels: 25.5 us -> 25.1 us  [on_device(): pl.pallas_call(kernel, out_shape=jax.ShapeDtypeStruct(queries.shape, bf),...]
where the time goes in v6:
time: 27 us; the launch traced here: 26.8 us
  Pallas kernels  25.1 us (93%)
  local copies, waits for them, and re-layouts  1.77 us (7%)
    pallas_call x1, Pallas kernels, on_device(): pl.pallas_call(kernel, out_shape=jax.ShapeDtypeStruct(queries.shape, bf),...  25.1 us
    unnamed x1, local copies, waits for them, and re-layouts  1.77 us

profile of v6, /device:TPU:163, one launch (start us, length us, event | category | flops | bytes accessed | tf_op | source)
XLA Modules:
  0.0 26.8 jit_solution(15819090180746193774)
XLA Ops:
  0.0 25.1 %shard_map.46 = bf16[2,64,1536]{2,1,0:T(8,128)(2,1)} custom-call(bf16[2,64,1536]{2,1,0:T(8,128)(2,1)} %q_hbm.1, bf16[2,64,1536]{2,1,0:T(8,128)(2,1)} %k_hbm.1, bf16[2,64,1536]{2,1,0:T(8,128)(2,1)} %v_hbm.1, s32[2]{0:T(128)} %clip_hbm.1), custom_call_target="tpu_custom_call" | custom-call | flops 1073741824 | bytes 4194304 | tf_op jit(solution)/shard_map/pallas_call | solution.py:606
  25.1 1.8 %copy.6 = bf16[2,64,1536]{2,1,0:T(8,128)(2,1)} copy(bf16[2,64,1536]{2,1,0:T(8,128)(2,1)} %shard_map.46) | data formatting | bytes 786432

commit v7 on v6

--- a/solution.py
+++ b/solution.py
@@ -176,17 +176,16 @@
                 for core in range(NC):
                     act(mixed(delta, core))
 
+    halves = []
+    for n, (src, dst) in enumerate(((k_hbm, kb), (v_hbm, vb), (q_hbm, qb))):
+        cp = remote(src.at[:, :, pl.ds(hi, HALF)], dst.at[mine], sib_ss.at[n], sib_rs.at[n], sibling)
+        cp.start()
+        halves.append(cp)
     each_rise(lambda cp: cp.start())
     each_mixed(lambda cp: cp.start())
     across = remote(pooled.at[1 - c], far.at[OWN, c], own_ss.at[0], own_rs.at[0], sibling)
     across.start()
     far[OWN, c] = pooled[c]
-
-    halves = []
-    for n, (src, dst) in enumerate(((k_hbm, kb), (v_hbm, vb), (q_hbm, qb))):
-        cp = remote(src.at[:, :, pl.ds(hi, HALF)], dst.at[mine], sib_ss.at[n], sib_rs.at[n], sibling)
-        cp.start()
-        halves.append(cp)
 
     def wait_half(n):
         local[n].wait()
@@ -207,19 +206,20 @@
         cp.start()
         level_sends.append(cp)
 
+    def near_out(n):
+        return remote(
+            near.at[n, pl.ds(4 * NEAR_ROWS, 2 * NEAR_ROWS)], near.at[n, pl.ds(0, 2 * NEAR_ROWS)],
+            near_ss.at[n], near_rs.at[n], jnp.minimum((chip + 1) * NC + c, NZ * NY * NC - 1),
+        )
+
     near_pool = pool_matrix(NEAR_ROWS * FPC, FPC, 2)
     for n, full in enumerate((kb, vb)):
         wait_half(n)
         near[n, 2 * NEAR_ROWS :] = nn(near_pool, full[...].reshape(ROWS, HALF)).astype(jnp.bfloat16)
 
-    near_out = remote(
-        near.at[:, pl.ds(4 * NEAR_ROWS, 2 * NEAR_ROWS)], near.at[:, pl.ds(0, 2 * NEAR_ROWS)],
-        near_ss.at[0], near_rs.at[0], jnp.minimum((chip + 1) * NC + c, NZ * NY * NC - 1),
-    )
-
-    @pl.when(chip < NZ * NY - 1)
-    def _():
-        near_out.start()
+        @pl.when(chip < NZ * NY - 1)
+        def _():
+            near_out(n).start()
 
     for n in range(1, NY * NC):
         ref = level_clips.at[lax.rem(row + NY * NC - n, NY * NC)]
@@ -440,8 +440,9 @@
 
     @pl.when(chip > 0)
     def _():
-        ref = near.at[:, pl.ds(0, 2 * NEAR_ROWS)]
-        remote(ref, ref, near_ss.at[0], near_rs.at[0], d).wait_recv()
+        for n in range(2):
+            ref = near.at[n, pl.ds(0, 2 * NEAR_ROWS)]
+            remote(ref, ref, near_ss.at[n], near_rs.at[n], d).wait_recv()
 
     chain_on(3)
 
@@ -589,7 +590,8 @@
 
     @pl.when(chip < NZ * NY - 1)
     def _():
-        near_out.wait_send()
+        for n in range(2):
+            near_out(n).wait_send()
 
     for k in ORDER:
         for delta in spread_to(k):
@@ -633,7 +635,7 @@
             dma((LEVELS + 2, NC)), dma((LEVELS + 2, NC)),
             dma((NY, NC)), dma((NY, NC)),
             dma((LEVELS + 2, 2 * NY)), dma((LEVELS + 2, 2 * NY)), dma((LEVELS + 2,)),
-            dma((1,)), dma((1,)),
+            dma((2,)), dma((2,)),
             dma((NY * NC,)), dma((NY * NC,)),
             dma((LEVELS + 2,)), dma((LEVELS + 2,)),
             dma((PAIRS,)), dma((PAIRS,)), dma((PAIRS,)),

time: 27 us -> 27.2 us (level)
  no operation moved by 1% of the time
where the time goes in v7:
time: 27.2 us; the launch traced here: 26.8 us
  Pallas kernels  25 us (92%)
  local copies, waits for them, and re-layouts  1.77 us (7%)
    pallas_call x1, Pallas kernels, on_device(): pl.pallas_call(kernel, out_shape=jax.ShapeDtypeStruct(queries.shape, bf),...  25 us
    unnamed x1, local copies, waits for them, and re-layouts  1.77 us

profile of v7, /device:TPU:163, one launch (start us, length us, event | category | flops | bytes accessed | tf_op | source)
XLA Modules:
  0.0 26.8 jit_solution(4533044010887674765)
XLA Ops:
  0.0 25.0 %shard_map.46 = bf16[2,64,1536]{2,1,0:T(8,128)(2,1)} custom-call(bf16[2,64,1536]{2,1,0:T(8,128)(2,1)} %q_hbm.1, bf16[2,64,1536]{2,1,0:T(8,128)(2,1)} %k_hbm.1, bf16[2,64,1536]{2,1,0:T(8,128)(2,1)} %v_hbm.1, s32[2]{0:T(128)} %clip_hbm.1), custom_call_target="tpu_custom_call" | custom-call | flops 1073741824 | bytes 4194304 | tf_op jit(solution)/shard_map/pallas_call | solution.py:608
  25.0 1.8 %copy.6 = bf16[2,64,1536]{2,1,0:T(8,128)(2,1)} copy(bf16[2,64,1536]{2,1,0:T(8,128)(2,1)} %shard_map.46) | data formatting | bytes 786432

commit v8 on v6

--- a/solution.py
+++ b/solution.py
@@ -163,7 +163,7 @@
         )
 
     def each_rise(act):
-        for k in (1, 5, 2):
+        for k in (5, 1, 2):
             @pl.when(z + k < NZ)
             def _():
                 for core in range(NC):

time: 27 us -> 27 us (level)
  no operation moved by 1% of the time
where the time goes in v8:
time: 27 us; the launch traced here: 26.8 us
  Pallas kernels  25.1 us (93%)
  local copies, waits for them, and re-layouts  1.77 us (7%)
    pallas_call x1, Pallas kernels, on_device(): pl.pallas_call(kernel, out_shape=jax.ShapeDtypeStruct(queries.shape, bf),...  25.1 us
    unnamed x1, local copies, waits for them, and re-layouts  1.77 us

profile of v8, /device:TPU:163, one launch (start us, length us, event | category | flops | bytes accessed | tf_op | source)
XLA Modules:
  0.0 26.8 jit_solution(10259228292947318192)
XLA Ops:
  0.0 25.1 %shard_map.46 = bf16[2,64,1536]{2,1,0:T(8,128)(2,1)} custom-call(bf16[2,64,1536]{2,1,0:T(8,128)(2,1)} %q_hbm.1, bf16[2,64,1536]{2,1,0:T(8,128)(2,1)} %k_hbm.1, bf16[2,64,1536]{2,1,0:T(8,128)(2,1)} %v_hbm.1, s32[2]{0:T(128)} %clip_hbm.1), custom_call_target="tpu_custom_call" | custom-call | flops 1073741824 | bytes 4194304 | tf_op jit(solution)/shard_map/pallas_call | solution.py:606
  25.1 1.8 %copy.6 = bf16[2,64,1536]{2,1,0:T(8,128)(2,1)} copy(bf16[2,64,1536]{2,1,0:T(8,128)(2,1)} %shard_map.46) | data formatting | bytes 786432
